TPU v7x, 512 devices: a whole 4x4x16 slice. The times are simulated.
512 devices in a mesh: dom: 128 (over z, x, y_lo), rep: 4 (over y_hi, core).
Axes of the slice: x: 4, y: 4 (y_hi: 2, y_lo: 2; y = y_hi * 2 + y_lo), z: 16, core: 2. Of those that a mesh axis runs over, the one named last changes fastest.
Arguments:
- entities: float32 [131072, 400], P(('dom', 'rep')), may hold values from -1.8 to 1.8
- ent_state: float32 [131072], P(('dom', 'rep')), may hold values from 0.01 to 0.1
- relations: float32 [2560, 400], P(('dom', 'rep')), may hold values from -3 to 3
- rel_state: float32 [2560], P(('dom', 'rep')), may hold values from 1 to 10
- src_rows: int32 [512, 256], P(('dom', 'rep')), may hold values from 0 to 255
- dst_rows: int32 [512, 256], P(('dom', 'rep')), may hold values from 0 to 1023
- rel_ids: int32 [512, 256], P(('dom', 'rep')), may hold values from 0 to 2559
- neg_src: int32 [512, 1000], P(('dom', 'rep')), may hold values from 0 to 255
- neg_dst: int32 [512, 1000], P(('dom', 'rep')), may hold values from 0 to 1023
- edge_count: int32 [512], P(('dom', 'rep')), may hold values from 64 to 256, as said below
Outputs:
- new_entities: float32 [131072, 400], P(('dom', 'rep'))
- new_ent_state: float32 [131072], P(('dom', 'rep'))
- new_relations: float32 [2560, 400], P(('dom', 'rep'))
- new_rel_state: float32 [2560], P(('dom', 'rep'))
Inputs may be any that keep to these rules, and one draw needn't show every extreme that they name: `edge_count`: live edge slots of each device; some device fills all 256 slots.
All inputs are finite; a program needn't handle non-finite values.
Results may differ from a plain program's by a relative error of at most 0.0048.
Values may be sent and summed in bfloat16 or wider, within the bound.
A program may use at most 64 MiB of HBM per device.

v0:
```python
import jax
import jax.numpy as jnp
from jax import lax
from jax.sharding import PartitionSpec as P


def shifted(value, axis, by):
    devices = lax.axis_size(axis)
    return lax.ppermute(value, axis, [(i, (i + by) % devices) for i in range(devices)])


def complex_mul(left, right):
    width = left.shape[-1] // 2
    left_re, left_im = (left[..., :width], left[..., width:])
    right_re, right_im = (right[..., :width], right[..., width:])
    return jnp.concatenate(
        [left_re * right_re - left_im * right_im, left_re * right_im + left_im * right_re], -1
    )


def conjugate(values):
    width = values.shape[-1] // 2
    return jnp.concatenate([values[..., :width], -values[..., width:]], -1)


def bucket_grads(
    own_rows, part_rows, rel_table, src_idx, dst_idx, rel_idx, nsrc_idx, ndst_idx, count
):
    slots = src_idx.shape[0]
    negatives = nsrc_idx.shape[0]
    sources = own_rows[src_idx].astype(jnp.float32)
    objects = part_rows[dst_idx].astype(jnp.float32)
    operators = rel_table[rel_idx].astype(jnp.float32)
    live = (jnp.arange(slots, dtype=jnp.int32) < count).astype(jnp.float32)
    queries = complex_mul(sources, operators)
    turned = complex_mul(conjugate(operators), objects)
    query_half = queries.astype(jnp.bfloat16)
    turned_half = turned.astype(jnp.bfloat16)
    neg_sources = own_rows[nsrc_idx]
    neg_objects = part_rows[ndst_idx]
    positive = jnp.sum(queries * objects, -1)
    grad_pos = -live * jax.nn.sigmoid(-positive)
    dst_scores = jnp.dot(query_half, neg_objects.T, preferred_element_type=jnp.float32)
    src_scores = jnp.dot(turned_half, neg_sources.T, preferred_element_type=jnp.float32)
    grad_dst = (live[:, None] * jax.nn.sigmoid(dst_scores) / negatives).astype(jnp.bfloat16)
    grad_src = (live[:, None] * jax.nn.sigmoid(src_scores) / negatives).astype(jnp.bfloat16)
    d_query = grad_pos[:, None] * objects + jnp.dot(
        grad_dst, neg_objects, preferred_element_type=jnp.float32
    )
    d_turned = grad_pos[:, None] * sources + jnp.dot(
        grad_src, neg_sources, preferred_element_type=jnp.float32
    )
    d_negobj = jnp.dot(grad_dst.T, query_half, preferred_element_type=jnp.float32)
    d_negsrc = jnp.dot(grad_src.T, turned_half, preferred_element_type=jnp.float32)
    d_source = complex_mul(conjugate(operators), d_query) + grad_pos[:, None] * turned
    d_object = grad_pos[:, None] * queries + complex_mul(operators, d_turned)
    d_operator = complex_mul(conjugate(sources), d_query) + complex_mul(
        objects, conjugate(d_turned)
    )
    src_term = jax.ops.segment_sum(d_source, src_idx, own_rows.shape[0]) + jax.ops.segment_sum(
        d_negsrc, nsrc_idx, own_rows.shape[0]
    )
    dst_term = jax.ops.segment_sum(d_object, dst_idx, part_rows.shape[0]) + jax.ops.segment_sum(
        d_negobj, ndst_idx, part_rows.shape[0]
    )
    rel_term = jax.ops.segment_sum(d_operator, rel_idx, rel_table.shape[0])
    return (src_term, dst_term.astype(jnp.bfloat16), rel_term)


def local(
    entities,
    ent_state,
    relations,
    rel_state,
    src_rows,
    dst_rows,
    rel_ids,
    neg_src,
    neg_dst,
    edge_count,
):
    halfway = lax.axis_size("dom") // 2
    groups = lax.axis_size("rep")
    own_count = entities.shape[0]
    own_rows = entities.astype(jnp.bfloat16)
    partner = shifted(own_rows, "dom", halfway)
    part_rows = lax.all_gather(partner, "rep", axis=0, tiled=True)
    rel_table = lax.all_gather(relations.astype(jnp.bfloat16), ("dom", "rep"), axis=0, tiled=True)
    src_term, dst_term, rel_term = bucket_grads(
        own_rows,
        part_rows,
        rel_table,
        src_rows[0],
        dst_rows[0],
        rel_ids[0],
        neg_src[0],
        neg_dst[0],
        edge_count[0],
    )
    blocks = dst_term.reshape(groups, own_count, entities.shape[1])
    arrived = shifted(blocks, "dom", halfway)
    pieces = lax.all_to_all(arrived, "rep", split_axis=0, concat_axis=0, tiled=True)
    incoming = jnp.sum(pieces.astype(jnp.float32), 0)
    ent_grad = src_term + incoming
    new_ent_state = ent_state + jnp.mean(ent_grad * ent_grad, -1)
    new_entities = entities - 0.5 * ent_grad / jnp.sqrt(new_ent_state)[:, None]
    rel_grad = lax.psum_scatter(rel_term, ("dom", "rep"), scatter_dimension=0, tiled=True)
    new_rel_state = rel_state + jnp.mean(rel_grad * rel_grad, -1)
    new_relations = relations - 0.5 * rel_grad / jnp.sqrt(new_rel_state)[:, None]
    return (new_entities, new_ent_state, new_relations, new_rel_state)


def solution(mesh):
    placed = (
        P(("dom", "rep"), None),
        P(("dom", "rep")),
        P(("dom", "rep"), None),
        P(("dom", "rep")),
        P(("dom", "rep"), None),
        P(("dom", "rep"), None),
        P(("dom", "rep"), None),
        P(("dom", "rep"), None),
        P(("dom", "rep"), None),
        P(("dom", "rep")),
    )
    return jax.shard_map(
        local,
        mesh=mesh,
        in_specs=placed,
        out_specs=(
            P(("dom", "rep"), None),
            P(("dom", "rep")),
            P(("dom", "rep"), None),
            P(("dom", "rep")),
        ),
        check_vma=False,
    )
```

profile of v0, /device:TPU:6, one launch (start us, length us, event | category | flops | bytes accessed | tf_op | source)
XLA Modules:
  0.0 1408.8 jit_solution(3091820463780263097)
XLA Ops:
  7.2 0.0 all-gather.3.cloned.1.call-start
  7.2 1.3 convert_bitcast_fusion
  8.5 0.0 all-gather.3.cloned.1.call-update
  8.6 0.0 all-reduce.3.cloned.1.call-start
  8.6 1.2 copy.51
  9.8 0.0 copy-start.11
  9.9 15.7 %collective-permute-start = (bf16[256,400]{1,0:T(8,128)(2,1)S(1)}, bf16[256,400]{1,0:T(8,128)(2,1)S(1)}, u32[]{:S(2)}, u32[]{:S(2)}) collective-permute-start(bf16[256,400]{1,0:T(8,128)(2,1)S(1)} %convert_element_type.46), channel_id=1, source_target_pairs={{0,256},{4,260},{8,264},{12,268},{16,272},{20,276},{24,280},{28,28... | collective-permute-start | bytes 614408 | tf_op jit(solution)/shard_map/ppermute | solution.py:9
  25.6 0.7 compare_select_fusion.3
  26.3 1.2 gather_fusion.1
  27.4 0.1 copy.43
  28.3 0.0 copy-start.13
  28.4 0.0 copy-start.12
  28.4 0.0 copy-start.10
  28.4 5.1 gather_fusion.4
  33.4 0.6 pad_clamp_fusion.4
  34.1 0.6 compare_convert_fusion
  34.7 11.9 all_gather.7
  46.6 1.2 gather_fusion.2
  47.7 0.1 copy.44
  47.9 0.8 convert_element_type.48
  48.7 5.1 gather_fusion.3
  53.8 776.5 %all-gather.3.cloned.1.call-done = bf16[512,5,400]{2,1,0:T(8,128)(2,1)} async-done(((bf16[1,5,400]{2,1,0:T(8,128)(2,1)}), bf16[512,5,400]{2,1,0:T(8,128)(2,1)}) %all-gather.3.cloned.1.call-update) | async-done | bytes 2048016 | tf_op jit(solution)/shard_map/all_gather | solution.py:88
  830.3 5.3 reshape.254
  835.6 2.0 gather_fusion
  837.6 1.2 copy.41
  838.8 1.1 multiply_subtract_fusion.5
  839.9 0.1 multiply_reduce_fusion.1
  840.0 0.5 fusion.12
  840.5 1.8 fusion.24
  842.3 0.5 multiply_add_fusion
  842.8 0.1 multiply_subtract_fusion.1
  842.9 0.6 copy-done
  843.5 0.5 fusion.13
  844.0 0.4 copy-done.6
  844.4 0.5 convolution_add_fusion
  844.9 0.5 copy-done.2
  845.4 0.1 multiply_subtract_fusion
  845.5 1.1 maximum_add_fusion
  846.6 1.0 copy.47
  847.6 3.3 scatter_custom_fusion.2
  850.9 8.7 scatter_custom_fusion.3
  859.6 2.9 add_convert_fusion
  862.5 1.5 copy.49
  864.0 12.0 collective-permute-start.1
  876.0 0.2 copy.52
  876.2 4.8 scatter_custom_fusion.4
  881.0 0.0 all-reduce.3.cloned.1.call-update
  881.1 53.3 %collective-permute-done.1 = bf16[4,256,400]{1,2,0:T(8,128)(2,1)} collective-permute-done((bf16[4,256,400]{1,2,0:T(8,128)(2,1)S(1)}, bf16[4,256,400]{1,2,0:T(8,128)(2,1)}, u32[]{:S(2)}, u32[]{:S(2)}) %collective-permute-start.1) | collective-permute-done | bytes 819232 | tf_op jit(solution)/shard_map/ppermute | solution.py:9
  934.4 10.6 all-to-all-start
  945.0 0.2 copy.45
  945.2 2.3 scatter_custom_fusion
  947.5 1.8 fusion.27
  949.3 7.4 scatter_custom_fusion.1
  956.7 2.4 all-to-all-done
  959.1 0.1 convert_reduce_fusion
  959.2 0.2 copy.50
  959.4 0.2 multiply_reduce_fusion
  959.6 0.6 fusion.35
  960.2 0.1 divide_subtract_fusion
  960.3 0.9 copy.53
  961.2 437.9 %all-reduce.3.cloned.1.call-done = f32[2560,400]{1,0:T(8,128)} async-done(((f32[2560,400]{1,0:T(8,128)}), f32[2560,400]{1,0:T(8,128)}) %all-reduce.3.cloned.1.call-update) | async-done | bytes 4096016
  1399.2 0.9 multiply_reduce_fusion.2
  1400.0 0.5 fusion.34
  1400.6 1.4 divide_subtract_fusion.1
  (40 shorter events, 0.2 us)
Async XLA Ops:
  7.2 823.1 %all-gather.3.cloned.1.call-start = ((), (), s32[]{:S(2)}) async-start(), calls=%async_computation.1 | async-start | bytes 4202496 | tf_op jit(solution)/shard_map/all_gather | solution.py:88
  8.6 1390.6 %all-reduce.3.cloned.1.call-start = ((), (), s32[]{:S(2)}) async-start(), calls=%async_computation.2 | async-start | bytes 10485760
  9.8 18.5 %copy-start.11 = (s32[1,1000]{1,0:T(1,128)S(1)}, s32[1,1000]{1,0:T(1,128)}, u32[]{:S(2)}) copy-start(s32[1,1000]{1,0:T(1,128)} %param.17) | copy-start | bytes 12004
  9.9 24.8 %collective-permute-start = (bf16[256,400]{1,0:T(8,128)(2,1)S(1)}, bf16[256,400]{1,0:T(8,128)(2,1)S(1)}, u32[]{:S(2)}, u32[]{:S(2)}) collective-permute-start(bf16[256,400]{1,0:T(8,128)(2,1)S(1)} %convert_element_type.46), channel_id=1, source_target_pairs={{0,256},{4,260},{8,264},{12,268},{16,272},{20,276},{24,280},{28,28... | collective-permute-start | bytes 614408 | tf_op jit(solution)/shard_map/ppermute | solution.py:9
  27.6 5.9 copy-start.5
  28.3 5.1 copy-start.13
  28.4 5.7 copy-start.12
  28.4 5.7 copy-start.10
  47.9 5.9 copy-start.3
  837.6 2.4 copy-start.4
  837.6 2.5 copy-start.1
  837.6 2.5 copy-start.16
  842.3 1.2 copy-start
  843.5 0.9 copy-start.6
  844.4 1.0 copy-start.2
  862.5 13.5 copy-start.8
  864.0 70.4 %collective-permute-start.1 = (bf16[4,256,400]{1,2,0:T(8,128)(2,1)S(1)}, bf16[4,256,400]{1,2,0:T(8,128)(2,1)}, u32[]{:S(2)}, u32[]{:S(2)}) collective-permute-start(bf16[4,256,400]{1,2,0:T(8,128)(2,1)S(1)} %copy.49), channel_id=1, source_target_pairs={{0,256},{4,260},{8,264},{12,268},{16,272},{20,276},{24,280},{28,28... | collective-permute-start | bytes 2457608 | tf_op jit(solution)/shard_map/ppermute | solution.py:9
  881.0 63.9 %copy-start.7 = (f32[256,400]{0,1:T(8,128)S(1)}, f32[256,400]{0,1:T(8,128)}, u32[]{:S(2)}) copy-start(f32[256,400]{0,1:T(8,128)} %get-tuple-element.38) | copy-start | bytes 1228804
  934.4 24.7 %all-to-all-start = ((bf16[4,256,400]{1,2,0:T(8,128)(2,1)}), bf16[4,256,400]{1,2,0:T(8,128)(2,1)S(1)}, u32[]{:S(2)}, u32[]{:S(2)}) async-start(bf16[4,256,400]{1,2,0:T(8,128)(2,1)} %collective-permute-done.1), calls=%async_computation | async-start | bytes 1638400 | tf_op jit(solution)/shard_map/all_to_all | solution.py:102
  949.3 10.3 copy-start.14
  959.6 440.5 %copy-start.15 = (f32[5]{0:T(128)S(1)}, f32[5]{0:T(128)}, u32[]{:S(2)}) copy-start(f32[5]{0:T(128)} %param.13) | copy-start | bytes 64
  959.6 441.0 %copy-start.9 = (f32[5,400]{1,0:T(8,128)S(1)}, f32[5,400]{1,0:T(8,128)}, u32[]{:S(2)}) copy-start(f32[5,400]{1,0:T(8,128)} %param.12) | copy-start | bytes 24004
Sparse Core Ops, SparseCore 0:
  10.8 819.4 all-gather.2
  881.2 517.9 all-reduce.2
where the time goes:
time: 1410 us
  waiting for transfers between devices  1270 us (90%)
  other arithmetic  39.9 us (3%)
  starting transfers between devices  38.3 us (3%)
  local copies, waits for them, and re-layouts  27.9 us (2%)
  between operations  15 us (1%)
    all_gather x1, waiting for transfers between devices, local(): lax.all_gather(relations.astype(jnp.bfloat16), ('dom', 'rep'), axis=0, ti...  777 us
    unnamed x3, waiting for transfers between devices  438 us
    ppermute x2, waiting for transfers between devices, shifted(): lax.ppermute(value, axis, [(i, (i + by) % devices) for i in range(devices)])  53.3 us
  transfers between devices with their start and end apart: 5, of which 4 were waited for; matrix products, arithmetic and copies ran while one was open for 3% of the time, Pallas kernels for 0%

commit v1 on v0

v1 whole, which is shorter than its diff:
```python
import jax
import jax.numpy as jnp
from jax import lax
from jax.experimental import pallas as pl
from jax.experimental.pallas import tpu as pltpu
from jax.sharding import PartitionSpec as P

Z, X, YL, YH, CORES = 16, 4, 2, 2, 2
Y = YL * YH
PI = X * Y
D = 400
HALF = D // 2
PAD = 512
ROWS = 256
EDGES = 256
NEG = 1000
NEG_PAD = 1024
REP = YH * CORES
REL_DEV = 5
TILE = 16
REL_ROWS = Z * TILE
CB = Z * REL_DEV
CHUNKS = 5
CH = D // CHUNKS
GROUP = min(4, PI)
GROUPS = PI // GROUP
STEP = 40
STEPS = HALF // STEP
SHIFT_PLANE = (PI * CORES).bit_length() - 1
SHIFT_CORE = CORES.bit_length() - 1
BF = jnp.bfloat16
F32 = jnp.float32
MESH = pl.DeviceIdType.MESH


def nn(a, b):
    return jnp.dot(a, b, preferred_element_type=F32)


def nt(a, b):
    return lax.dot_general(a, b, (((1,), (1,)), ((), ())), preferred_element_type=F32)


def iota(shape, dim):
    return lax.broadcasted_iota(jnp.int32, shape, dim)


def one_hot(cond):
    return jnp.where(cond, 1.0, 0.0).astype(BF)


def div5(v):
    return lax.shift_right_logical(v * 52429, 18)


def remote(src, dst, send, recv, peer):
    return pltpu.make_async_remote_copy(
        src_ref=src, dst_ref=dst, send_sem=send, recv_sem=recv, device_id=peer, device_id_type=MESH
    )


def kernel(
    ent, state, rel, rel_state, src_rows, dst_rows, rel_ids, neg_src, neg_dst, count,
    new_ent, new_state, new_rel, new_rel_state,
    eb, part, zt, g, tf, ohs, ohd, ohx, ohz, ohxt, ohzt, negs, cnts,
    sf, wf, of, qf, uf, dqf, dpf, dof, dsf, dwf,
    qb, qrow, urow, gmat, gs, dob, dwb, dwz,
    dest, dcr, ysend, yrecv, ezs, ezr, rblk, rcr, rpr, zsend, zrecv,
    zt_s, zt_r, e_s, e_r, y_s, y_r, c1_s, c1_r, c2_s, c2_r, p_s, p_r, g_s, g_r,
    dc_s, dc_r, dy_s, dy_r, dz_s, dz_r, rc_s, rc_r, rp_s, rp_r, rz_s, rz_r,
):
    dom = lax.axis_index("dom")
    rep = lax.axis_index("rep")
    z = dom // (X * YL)
    x = (dom // YL) % X
    yl = dom % YL
    yh = rep // CORES
    c = rep % CORES
    y = yh * YL + yl
    cm = 1 - c
    pi = (x * YL + yl) * YH + yh

    def device(dz, dx, dy, core):
        yy = (y + dy) % Y
        return {
            "dom": (((z + dz) % Z) * X + (x + dx) % X) * YL + yy % YL,
            "rep": (yy // YL) * CORES + core,
        }

    def plane_peer(n):
        return device(0, n // Y, n % Y, c)

    def plane_index(n):
        yy = (y + n % Y) % Y
        return (((x + n // Y) % X) * YL + yy % YL) * YH + yy // YL

    def plane_from(n):
        yy = (y + Y - n % Y) % Y
        return (((x + X - n // Y) % X) * YL + yy % YL) * YH + yy // YL

    mate = device(0, 0, 0, cm)
    across = device(0, 0, YL, c)
    far = device(Z // 2, 0, 0, c)

    barrier = pltpu.get_barrier_semaphore()

    @pl.loop(1, Z)
    def _(n):
        pl.semaphore_signal(barrier, inc=1, device_id=device(n, 0, 0, c), device_id_type=MESH)

    @pl.loop(1, PI)
    def _(n):
        pl.semaphore_signal(barrier, inc=1, device_id=plane_peer(n), device_id_type=MESH)

    pl.semaphore_signal(barrier, inc=1, device_id=mate, device_id_type=MESH)

    eb[0:D, :] = ent[...].astype(BF)
    lane = iota((REL_DEV, 128), 1)
    row5 = iota((REL_DEV, 128), 0)
    for k in range(3):
        tf[k * REL_DEV : (k + 1) * REL_DEV, :] = rel[:, k * 128 : (k + 1) * 128]
    spread16 = one_hot((iota((16, 128), 1) & 15) == iota((16, 128), 0))
    last = nn(rel[:, 384:400].astype(BF), spread16)
    last = jnp.where(lax.shift_right_logical(lane, 4) == row5, last, 0.0)
    tf[15:16, :] = jnp.sum(last, axis=0, keepdims=True)
    own_tile = pl.ds(pl.multiple_of(z * TILE, TILE), TILE)
    zt[own_tile, :] = tf[...].astype(BF)

    pl.semaphore_wait(barrier, (Z - 1) + (PI - 1) + 1)

    def tile_copy(n):
        return remote(zt.at[own_tile], zt.at[own_tile], zt_s.at[n], zt_r.at[n], device(n, 0, 0, c))

    @pl.loop(1, Z)
    def _(n):
        tile_copy(n).start()

    def rows_of(k):
        return pl.ds(k * CH, CH)

    ent_copies = [
        remote(eb.at[rows_of(k)], part.at[rep, rows_of(k)], e_s.at[k], e_r.at[k], far)
        for k in range(CHUNKS)
    ]
    for k in range(CHUNKS):
        ent_copies[k].start()

    part[:, D:PAD, :] = jnp.zeros((REP, PAD - D, ROWS), BF)
    eb[D:PAD, :] = jnp.zeros((PAD - D, ROWS), BF)
    qf[D:PAD, :] = jnp.zeros((PAD - D, EDGES), F32)
    uf[D:PAD, :] = jnp.zeros((PAD - D, EDGES), F32)
    dwf[D:PAD, :] = jnp.zeros((PAD - D, EDGES), F32)
    ids = rel_ids[...]
    owner = div5(ids)
    slot = ids - owner * REL_DEV
    owner_z = lax.shift_right_logical(owner, SHIFT_PLANE)
    owner_p = owner & (PI * CORES - 1)
    block = (owner_p & (CORES - 1)) * PI + lax.shift_right_logical(owner_p, SHIFT_CORE)
    pos = block * CB + owner_z * REL_DEV + slot
    posz = block * Z + owner_z

    ohs[...] = one_hot(iota((ROWS, EDGES), 0) == src_rows[...])
    for b in range(REP):
        ohd[b] = one_hot(iota((ROWS, EDGES), 0) + b * ROWS == dst_rows[...])

    def column(row):
        return jnp.transpose(jnp.broadcast_to(row.astype(F32), (EDGES, EDGES)))[:, :128]

    pos_col = column(pos)
    posz_col = column(posz)
    slot_col = column(slot)
    blocks = PI * CORES

    @pl.loop(0, CORES)
    def _(k):
        @pl.loop(0, PI)
        def _(n):
            at = k * PI + n
            ohx[k, pl.ds(pl.multiple_of(n * CB, 16), CB), :] = one_hot(
                iota((CB, EDGES), 0) + at * CB == pos
            )
            ohz[k, pl.ds(pl.multiple_of(n * Z, 16), Z), :] = one_hot(
                iota((Z, EDGES), 0) + at * Z == posz
            )

    lanes = iota((EDGES, 128), 1).astype(F32)
    for t in range(0, blocks * CB, 128):
        hot = one_hot(lanes + float(t) == pos_col)
        ohxt[:, t : t + 128] = hot[:, : min(128, blocks * CB - t)]
    for t in range(0, blocks * Z, 128):
        hot = one_hot(lanes + float(t) == posz_col)
        ohzt[:, t : t + 128] = hot[:, : min(128, blocks * Z - t)]
    slot_mask = lax.shift_right_logical(iota((EDGES, 128), 1), 4).astype(F32) == slot_col

    ones = jnp.ones((16, NEG_PAD), BF)
    negs[...] = jnp.full((2, NEG_PAD), -1, jnp.int32)
    negs[0:1, 0:NEG] = neg_dst[...]
    negs[1:2, 0:NEG] = neg_src[...]
    for b in range(REP):
        cnts[b] = nt(ones, one_hot(iota((ROWS, NEG_PAD), 0) + b * ROWS == negs[0:1, :]))
    cnts[REP] = nt(ones, one_hot(iota((ROWS, NEG_PAD), 0) == negs[1:2, :]))
    sf[...] = nn(eb[0:D, :], ohs[...])

    def plane_copy(n):
        return remote(g.at[c, pi], g.at[c, pi], p_s.at[n], p_r.at[n], plane_peer(n))

    def plane_arrival(n):
        came = plane_from(n)
        return remote(g.at[c, came], g.at[c, came], p_s.at[n], p_r.at[n], plane_peer(n))

    def core_copy(n):
        came = plane_from(n)
        return remote(g.at[c, came], g.at[c, came], g_s.at[n], g_r.at[n], mate)

    def core_arrival(n):
        came = plane_from(n)
        return remote(g.at[cm, came], g.at[cm, came], g_s.at[n], g_r.at[n], mate)

    @pl.loop(1, Z)
    def _(n):
        came = pl.ds(pl.multiple_of(((z + Z - n) % Z) * TILE, TILE), TILE)
        remote(zt.at[came], zt.at[came], zt_s.at[n], zt_r.at[n], device(n, 0, 0, c)).wait_recv()

    def by_kind(k):
        zz = lax.shift_right_logical(k, 4)
        s = k & 15
        kind = lax.shift_right_logical(s * 13, 6)
        return kind * CB + jnp.where(kind < 3, zz * REL_DEV + s - kind * REL_DEV, zz)

    square = (REL_ROWS, REL_ROWS)
    g[c, pi] = nn(one_hot(iota(square, 0) == by_kind(iota(square, 1))), zt[...]).astype(BF)

    @pl.loop(1, PI)
    def _(n):
        plane_copy(n).start()

    core_copy(0).start()

    y_copies = [
        remote(part.at[rep, rows_of(k)], part.at[rep, rows_of(k)], y_s.at[k], y_r.at[k], across)
        for k in range(CHUNKS)
    ]
    c1_copies = [
        remote(part.at[rep, rows_of(k)], part.at[rep, rows_of(k)], c1_s.at[k], c1_r.at[k], mate)
        for k in range(CHUNKS)
    ]
    rep_y = (1 - yh) * CORES + c
    rep_m = yh * CORES + cm
    rep_d = (1 - yh) * CORES + cm
    c2_copies = [
        remote(part.at[rep_y, rows_of(k)], part.at[rep_y, rows_of(k)], c2_s.at[k], c2_r.at[k], mate)
        for k in range(CHUNKS)
    ]

    def arrival(k, at, sends, recvs, peer):
        return remote(part.at[at, rows_of(k)], part.at[at, rows_of(k)], sends.at[k], recvs.at[k], peer)

    share = -(-(PI - 1) // CHUNKS)
    for k in range(CHUNKS):
        ent_copies[k].wait_recv()
        y_copies[k].start()
        c1_copies[k].start()

        @pl.loop(1 + k * share, min(PI, 1 + (k + 1) * share))
        def _(n):
            plane_arrival(n).wait_recv()
            core_copy(n).start()

    for k in range(CHUNKS):
        arrival(k, rep_y, y_s, y_r, across).wait_recv()
        c2_copies[k].start()

    @pl.loop(0, PI)
    def _(n):
        core_arrival(n).wait_recv()

    table = g[...].reshape(blocks, REL_ROWS, 128)
    for k in range(3):
        w = nn(ohxt[...], table[:, k * CB : (k + 1) * CB, :].reshape(blocks * CB, 128))
        wf[k * 128 : (k + 1) * 128, :] = jnp.transpose(w)
    w = nn(ohzt[...], table[:, 3 * CB :, :].reshape(blocks * Z, 128))
    fold = one_hot(
        ((iota((128, 128), 0) & 15) == iota((128, 128), 1)) & (iota((128, 128), 0) < 16 * REL_DEV)
    )
    w = nn(jnp.where(slot_mask, w, 0.0).astype(BF), fold)
    wf[384:512, :] = jnp.transpose(w)

    def parts(ref, k):
        re = pl.ds(pl.multiple_of(k * STEP, 8), STEP)
        im = pl.ds(pl.multiple_of(HALF + k * STEP, 8), STEP)
        return ref[re, :], ref[im, :]

    def put(ref, k, re_value, im_value):
        ref[pl.ds(pl.multiple_of(k * STEP, 8), STEP), :] = re_value
        ref[pl.ds(pl.multiple_of(HALF + k * STEP, 8), STEP), :] = im_value

    @pl.loop(0, STEPS)
    def _(k):
        s_re, s_im = parts(sf, k)
        w_re, w_im = parts(wf, k)
        put(qf, k, s_re * w_re - s_im * w_im, s_re * w_im + s_im * w_re)

    qb[...] = qf[0:D, :].astype(BF)
    for k in range(PAD // 128):
        at = slice(k * 128, (k + 1) * 128)
        qrow[:, at] = jnp.transpose(qf[at, :]).astype(BF)

    for k in range(CHUNKS):
        arrival(k, rep_m, c1_s, c1_r, mate).wait_recv()
        arrival(k, rep_d, c2_s, c2_r, mate).wait_recv()

    total = nn(part[0, 0:D, :], ohd[0])
    for b in range(1, REP):
        total += nn(part[b, 0:D, :], ohd[b])
    of[...] = total

    def turn(k, positive):
        w_re, w_im = parts(wf, k)
        o_re, o_im = parts(of, k)
        q_re, q_im = parts(qf, k)
        put(uf, k, w_re * o_re + w_im * o_im, w_re * o_im - w_im * o_re)
        return positive + jnp.sum(q_re * o_re + q_im * o_im, axis=0, keepdims=True)

    positive = lax.fori_loop(0, STEPS, turn, jnp.zeros((1, EDGES), F32))
    live = count[...]
    live_row = jnp.where(iota((1, EDGES), 1) < live, 1.0, 0.0)
    live_col = jnp.where(iota((EDGES, 1), 0) < live, 1.0 / NEG, 0.0)
    grad_pos = -live_row * jax.nn.sigmoid(-positive)

    for k in range(PAD // 128):
        at = slice(k * 128, (k + 1) * 128)
        urow[:, at] = jnp.transpose(uf[at, :]).astype(BF)

    def weights(scores, b):
        return (jax.nn.sigmoid(scores) * cnts[b, 0:1, :] * live_col).astype(BF)

    gs[...] = weights(nn(urow[...], eb[...]), REP)
    for b in range(REP):
        gmat[b] = weights(nn(qrow[...], part[b]), b)
    dpf[...] = nt(eb[0:D, :], gs[...])
    total = nt(part[0, 0:D, :], gmat[0])
    for b in range(1, REP):
        total += nt(part[b, 0:D, :], gmat[b])
    dqf[...] = total

    @pl.loop(0, STEPS)
    def _(k):
        s_re, s_im = parts(sf, k)
        w_re, w_im = parts(wf, k)
        o_re, o_im = parts(of, k)
        q_re, q_im = parts(qf, k)
        u_re, u_im = parts(uf, k)
        dq_re, dq_im = parts(dqf, k)
        dp_re, dp_im = parts(dpf, k)
        dq_re += grad_pos * o_re
        dq_im += grad_pos * o_im
        dp_re += grad_pos * s_re
        dp_im += grad_pos * s_im
        put(
            dof, k,
            grad_pos * q_re + w_re * dp_re - w_im * dp_im,
            grad_pos * q_im + w_re * dp_im + w_im * dp_re,
        )
        put(
            dwf, k,
            s_re * dq_re + s_im * dq_im + o_re * dp_re + o_im * dp_im,
            s_re * dq_im - s_im * dq_re + o_im * dp_re - o_re * dp_im,
        )
        put(
            dsf, k,
            w_re * dq_re + w_im * dq_im + grad_pos * u_re,
            w_re * dq_im - w_im * dq_re + grad_pos * u_im,
        )

    dob[...] = dof[...].astype(BF)

    def dc_copy(k):
        return remote(
            dest.at[cm, :, rows_of(k)], dcr.at[:, rows_of(k)], dc_s.at[k], dc_r.at[k], mate
        )

    def dy_copy(k):
        return remote(ysend.at[rows_of(k)], yrecv.at[rows_of(k)], dy_s.at[k], dy_r.at[k], across)

    def dz_copy(k):
        return remote(ezs.at[rows_of(k)], ezr.at[rows_of(k)], dz_s.at[k], dz_r.at[k], far)

    for k in range(CHUNKS):
        at = slice(k * CH, (k + 1) * CH)
        for b in range(REP):
            dest[b % CORES, b // CORES, at, :] = (
                nn(qb[at, :], gmat[b]) + nt(dob[at, :], ohd[b])
            ).astype(BF)
        dc_copy(k).start()

    for k in range(3):
        dwb[:, k * 128 : (k + 1) * 128] = jnp.transpose(dwf[k * 128 : (k + 1) * 128, :]).astype(BF)
    spread = one_hot(
        ((iota((128, 128), 1) & 15) == iota((128, 128), 0)) & (iota((128, 128), 1) < 16 * REL_DEV)
    )
    tail = nn(jnp.transpose(dwf[384:512, :]).astype(BF), spread)
    dwz[...] = jnp.where(slot_mask, tail, 0.0).astype(BF)

    def rel_blocks(core, n):
        rows = nn(ohx[core, n * GROUP * CB : (n + 1) * GROUP * CB, :], dwb[...]).astype(BF)
        ends = nn(ohz[core, n * GROUP * Z : (n + 1) * GROUP * Z, :], dwz[...]).astype(BF)
        for m in range(GROUP):
            for k in range(3):
                rblk[core, n * GROUP + m, k * CB : (k + 1) * CB, :] = rows[
                    m * CB : (m + 1) * CB, k * 128 : (k + 1) * 128
                ]
            rblk[core, n * GROUP + m, 3 * CB :, :] = ends[m * Z : (m + 1) * Z, :]

    def rc_copy(n):
        at = pl.ds(n * GROUP, GROUP)
        return remote(rblk.at[cm, at], rcr.at[at], rc_s.at[n], rc_r.at[n], mate)

    for n in range(GROUPS):
        rel_blocks(cm, n)
        rc_copy(n).start()

    for k in range(CHUNKS):
        at = slice(k * CH, (k + 1) * CH)
        dc_copy(k).wait_recv()
        ysend[at, :] = (dest[c, 1 - yh, at, :].astype(F32) + dcr[1 - yh, at, :].astype(F32)).astype(BF)
        dy_copy(k).start()

    for n in range(GROUPS):
        rel_blocks(c, n)

    for k in range(CHUNKS):
        at = slice(k * CH, (k + 1) * CH)
        dy_copy(k).wait_recv()
        ezs[at, :] = (
            dest[c, yh, at, :].astype(F32)
            + dcr[yh, at, :].astype(F32)
            + yrecv[at, :].astype(F32)
        ).astype(BF)
        dz_copy(k).start()

    for n in range(GROUPS):
        rc_copy(n).wait_recv()

    def rp_copy(n):
        return remote(rblk.at[c, plane_index(n)], rpr.at[n], rp_s.at[n], rp_r.at[n], plane_peer(n))

    def both(at):
        return rblk[c, at].astype(F32) + rcr[at].astype(F32)

    @pl.loop(1, PI)
    def _(n):
        at = plane_index(n)
        rblk[c, at] = both(at).astype(BF)
        rp_copy(n).start()

    ds_hi = dsf[...].astype(BF)
    ds_lo = (dsf[...] - ds_hi.astype(F32)).astype(BF)
    uhalf = uf[0:D, :].astype(BF)
    sf[...] = nn(uhalf, gs[...]) + nt(ds_hi, ohs[...]) + nt(ds_lo, ohs[...])

    def add_plane(n, acc):
        rp_copy(n).wait_recv()
        return acc + rpr[n].astype(F32)

    plane_sum = lax.fori_loop(1, PI, add_plane, both(pi))
    to_z = one_hot(iota(square, 1) == by_kind(iota(square, 0)))
    zsend[...] = nn(to_z, plane_sum.astype(BF)).astype(BF)

    def rz_copy(n):
        at = pl.ds(pl.multiple_of(((z + n) % Z) * TILE, TILE), TILE)
        return remote(zsend.at[at], zrecv.at[n], rz_s.at[n], rz_r.at[n], device(n, 0, 0, c))

    @pl.loop(1, Z)
    def _(n):
        rz_copy(n).start()

    for k in range(CHUNKS):
        dz_copy(k).wait_recv()
    ent_grad = sf[...] + ezr[...].astype(F32)
    fresh = state[...] + jnp.sum(ent_grad * ent_grad, axis=0, keepdims=True) * (1.0 / D)
    new_state[...] = fresh
    new_ent[...] = ent[...] - ent_grad * (0.5 / jnp.sqrt(fresh))

    def add_tile(n, acc):
        rz_copy(n).wait_recv()
        return acc + zrecv[n].astype(F32)

    tf[...] = lax.fori_loop(1, Z, add_tile, zsend[own_tile, :].astype(F32))
    own_slot = lax.shift_right_logical(lane, 4) == row5
    ends = jnp.where(own_slot, jnp.broadcast_to(tf[15:16, :], (REL_DEV, 128)), 0.0)
    fold_f = fold.astype(F32)
    ends = jnp.dot(ends, fold_f, precision=lax.Precision.HIGHEST, preferred_element_type=F32)
    pieces = [tf[k * REL_DEV : (k + 1) * REL_DEV, :] for k in range(3)] + [ends]
    squares = jnp.sum(sum(piece * piece for piece in pieces), axis=1, keepdims=True)
    eye = iota((REL_DEV, REL_DEV), 0) == iota((REL_DEV, REL_DEV), 1)
    old = jnp.broadcast_to(rel_state[...], (REL_DEV, REL_DEV))
    old = jnp.sum(jnp.where(eye, old, 0.0), axis=1, keepdims=True)
    fresh = old + squares * (1.0 / D)
    new_rel_state[...] = jnp.sum(
        jnp.where(eye, jnp.broadcast_to(fresh, (REL_DEV, REL_DEV)), 0.0), axis=0, keepdims=True
    )
    scale = 0.5 / jnp.sqrt(fresh)
    for k in range(3):
        at = slice(k * 128, (k + 1) * 128)
        new_rel[:, at] = rel[:, at] - pieces[k] * scale
    new_rel[:, 384:400] = rel[:, 384:400] - ends[:, 0:16] * scale

    for k in range(CHUNKS):
        ent_copies[k].wait_send()
        y_copies[k].wait_send()
        c1_copies[k].wait_send()
        c2_copies[k].wait_send()
        dc_copy(k).wait_send()
        dy_copy(k).wait_send()
        dz_copy(k).wait_send()
    for n in range(GROUPS):
        rc_copy(n).wait_send()
    core_copy(0).wait_send()

    @pl.loop(1, Z)
    def _(n):
        tile_copy(n).wait_send()
        rz_copy(n).wait_send()

    @pl.loop(1, PI)
    def _(n):
        plane_copy(n).wait_send()
        core_copy(n).wait_send()
        rp_copy(n).wait_send()


def scratch():
    vm = pltpu.VMEM
    dma = pltpu.SemaphoreType.DMA
    blocks = PI * CORES
    return [
        vm((PAD, ROWS), BF),
        vm((REP, PAD, ROWS), BF),
        vm((REL_ROWS, 128), BF),
        vm((CORES, PI, REL_ROWS, 128), BF),
        vm((TILE, 128), F32),
        vm((ROWS, EDGES), BF),
        vm((REP, ROWS, EDGES), BF),
        vm((CORES, PI * CB, EDGES), BF),
        vm((CORES, PI * Z, EDGES), BF),
        vm((EDGES, blocks * CB), BF),
        vm((EDGES, blocks * Z), BF),
        vm((2, NEG_PAD), jnp.int32),
        vm((REP + 1, 16, ROWS), F32),
        vm((D, EDGES), F32),
        vm((PAD, EDGES), F32),
        vm((D, EDGES), F32),
        vm((PAD, EDGES), F32),
        vm((PAD, EDGES), F32),
        vm((D, EDGES), F32),
        vm((D, EDGES), F32),
        vm((D, EDGES), F32),
        vm((D, EDGES), F32),
        vm((PAD, EDGES), F32),
        vm((D, EDGES), BF),
        vm((EDGES, PAD), BF),
        vm((EDGES, PAD), BF),
        vm((REP, EDGES, ROWS), BF),
        vm((EDGES, ROWS), BF),
        vm((D, EDGES), BF),
        vm((EDGES, 384), BF),
        vm((EDGES, 128), BF),
        vm((CORES, YH, D, ROWS), BF),
        vm((YH, D, ROWS), BF),
        vm((D, ROWS), BF),
        vm((D, ROWS), BF),
        vm((D, ROWS), BF),
        vm((D, ROWS), BF),
        vm((CORES, PI, REL_ROWS, 128), BF),
        vm((PI, REL_ROWS, 128), BF),
        vm((PI, REL_ROWS, 128), BF),
        vm((REL_ROWS, 128), BF),
        vm((Z, TILE, 128), BF),
        dma((Z,)), dma((Z,)),
        dma((CHUNKS,)), dma((CHUNKS,)),
        dma((CHUNKS,)), dma((CHUNKS,)),
        dma((CHUNKS,)), dma((CHUNKS,)),
        dma((CHUNKS,)), dma((CHUNKS,)),
        dma((PI,)), dma((PI,)),
        dma((PI,)), dma((PI,)),
        dma((CHUNKS,)), dma((CHUNKS,)),
        dma((CHUNKS,)), dma((CHUNKS,)),
        dma((CHUNKS,)), dma((CHUNKS,)),
        dma((GROUPS,)), dma((GROUPS,)),
        dma((PI,)), dma((PI,)),
        dma((Z,)), dma((Z,)),
    ]


def local(
    entities, ent_state, relations, rel_state, src_rows, dst_rows, rel_ids, neg_src, neg_dst, edge_count
):
    vmem = pl.BlockSpec(memory_space=pltpu.VMEM)
    new_ent, new_state, new_rel, new_rel_state = pl.pallas_call(
        kernel,
        out_shape=(
            jax.ShapeDtypeStruct((D, ROWS), F32),
            jax.ShapeDtypeStruct((1, ROWS), F32),
            jax.ShapeDtypeStruct((REL_DEV, D), F32),
            jax.ShapeDtypeStruct((1, REL_DEV), F32),
        ),
        in_specs=[vmem] * 10,
        out_specs=(vmem,) * 4,
        scratch_shapes=scratch(),
        compiler_params=pltpu.CompilerParams(
            collective_id=0, has_side_effects=True, vmem_limit_bytes=56 * 1024 * 1024
        ),
        name="bucket_round",
    )(
        entities.T,
        ent_state.reshape(1, ROWS),
        relations,
        rel_state.reshape(1, REL_DEV),
        src_rows,
        dst_rows,
        rel_ids,
        neg_src,
        neg_dst,
        edge_count.reshape(1, 1),
    )
    return (new_ent.T, new_state.reshape(ROWS), new_rel, new_rel_state.reshape(REL_DEV))


def solution(mesh):
    rows = P(("dom", "rep"), None)
    flat = P(("dom", "rep"))
    return jax.shard_map(
        local,
        mesh=mesh,
        in_specs=(rows, flat, rows, flat, rows, rows, rows, rows, rows, flat),
        out_specs=(rows, flat, rows, flat),
        check_vma=False,
    )
```

time: 1410 us -> 93.7 us (0.07)
  waiting for transfers between devices: 1270 us -> 0 us
  Pallas kernels: 0 us -> 87.2 us
  other arithmetic: 39.9 us -> 0 us
  starting transfers between devices: 38.3 us -> 0 us
  local copies, waits for them, and re-layouts: 27.9 us -> 3.5 us
    all_gather x1 -> x0, waiting for transfers between devices: 777 us -> none  [local(): lax.all_gather(relations.astype(jnp.bfloat16), ('dom', 'rep'), axis=0, ti...]
    unnamed x3 -> x0, waiting for transfers between devices: 438 us -> none
    pallas_call x0 -> x1, Pallas kernels: none -> 87.2 us  [local(): pl.pallas_call(kernel, out_shape=(jax.ShapeDtypeStruct((D, ROWS), F32), j...]
    ppermute x2 -> x0, waiting for transfers between devices: 53.3 us -> none  [shifted(): lax.ppermute(value, axis, [(i, (i + by) % devices) for i in range(devices)])]
    ppermute x2 -> x0, starting transfers between devices: 27.7 us -> none  [shifted(): lax.ppermute(value, axis, [(i, (i + by) % devices) for i in range(devices)])]
    scatter-add x5 -> x0, other arithmetic: 26.5 us -> none  [the longest x1 8.67 us: bucket_grads(): jax.ops.segment_sum(d_negobj, ndst_idx, part_rows.shape[0])]
    gather x8 -> x0, local copies, waits for them, and re-layouts: 15.9 us -> none  [the longest x1 5.09 us: bucket_grads(): neg_objects = part_rows[ndst_idx]]
  transfers between devices with their start and end apart: 5 -> 0, of which waited for: 4 -> 0; matrix products, arithmetic and copies ran while one was open for 3% -> 0% of each run, Pallas kernels for 0% -> 0%
where the time goes in v1:
time: 93.7 us; the launch traced here: 92.1 us
  Pallas kernels  87.2 us (93%)
  local copies, waits for them, and re-layouts  3.5 us (4%)
  between operations  1.31 us (1%)
    pallas_call x1, Pallas kernels, local(): pl.pallas_call(kernel, out_shape=(jax.ShapeDtypeStruct((D, ROWS), F32), j...  87.2 us
    unnamed x10, local copies, waits for them, and re-layouts  3.5 us

profile of v1, /device:TPU:6, one launch (start us, length us, event | category | flops | bytes accessed | tf_op | source)
XLA Modules:
  0.0 92.1 jit_solution(14306312835065047229)
XLA Ops:
  1.3 87.2 %bucket_round.1 = (f32[400,256]{1,0:T(8,128)}, f32[1,256]{1,0:T(1,128)}, f32[5,400]{1,0:T(8,128)}, f32[1,5]{1,0:T(1,128)}) custom-call(f32[400,256]{1,0:T(8,128)} %bitcast.8, f32[1,256]{1,0:T(1,128)} %bitcast.10, f32[5,400]{1,0:T(8,128)} %rel.1, f32[1,5]{1,0:T(1,128)} %bitcast.12, s32[1,256]{1,0:T(1,128)} %src_rows.1, s32[1,256]{1,0:T(1,128)} %dst_rows.1, ...), custom_call_target="tpu_custom_call" | custom-call | tf_op jit(solution)/shard_map/bucket_round/pallas_call | solution.py:599
  88.5 0.0 copy-start.1
  88.5 0.0 copy-start
  88.5 1.8 %copy.19 = f32[256,400]{0,1:T(8,128)} copy(f32[256,400]{0,1:T(8,128)} %bitcast.9) | data formatting | bytes 819200
  90.3 0.0 copy-done.1
  90.3 0.6 copy.20
  90.9 0.0 copy-done
  90.9 0.0 copy-start.2
  90.9 0.6 copy.21
  91.5 0.0 copy-done.2
  91.5 0.5 copy.22
Async XLA Ops:
  88.5 1.8 %copy-start.1 = (f32[1,256]{1,0:T(1,128)S(1)}, f32[1,256]{1,0:T(1,128)}, u32[]{:S(2)}) copy-start(f32[1,256]{1,0:T(1,128)} %get-tuple-element.9) | copy-start | bytes 3076
  88.5 2.4 %copy-start = (f32[5,400]{1,0:T(8,128)S(1)}, f32[5,400]{1,0:T(8,128)}, u32[]{:S(2)}) copy-start(f32[5,400]{1,0:T(8,128)} %get-tuple-element.18) | copy-start | bytes 24004
  90.9 0.6 copy-start.2

commit v2 on v1

v2 whole, which is shorter than its diff:
```python
import jax
import jax.numpy as jnp
from jax import lax
from jax.experimental import pallas as pl
from jax.experimental.pallas import tpu as pltpu
from jax.sharding import PartitionSpec as P

Z, X, YL, YH, CORES = 16, 4, 2, 2, 2
Y = YL * YH
PI = X * Y
D = 400
HALF = D // 2
PAD = 512
ROWS = 256
EDGES = 256
NEG = 1000
NEG_PAD = 1024
REP = YH * CORES
REL_DEV = 5
TILE = 16
SLOTS = Z * TILE
CB = Z * REL_DEV
NR = 2 * Z
FR = CB - NR
NEAR_Z = -(-NR // REL_DEV)
NEAR_ROWS = 3 * NR
FAR_ROWS = 3 * FR + Z
FH = FAR_ROWS // 2
HALVES = ROWS // 128
SPLIT = 208
PIECES = [(at, size, h) for h in range(HALVES) for at, size in ((0, SPLIT), (SPLIT, D - SPLIT))]
CHUNKS = len(PIECES)
PER_HALF = CHUNKS // HALVES
STEP = 40
STEPS = HALF // STEP
SHIFT_PLANE = (PI * CORES).bit_length() - 1
SHIFT_CORE = CORES.bit_length() - 1
SHIFT_YH = SHIFT_CORE + YH.bit_length() - 1
SHIFT_YL = SHIFT_YH + YL.bit_length() - 1
BF = jnp.bfloat16
F32 = jnp.float32
MESH = pl.DeviceIdType.MESH


def nn(a, b):
    return jnp.dot(a, b, preferred_element_type=F32)


def nt(a, b):
    return lax.dot_general(a, b, (((1,), (1,)), ((), ())), preferred_element_type=F32)


def iota(shape, dim):
    return lax.broadcasted_iota(jnp.int32, shape, dim)


def one_hot(cond):
    return jnp.where(cond, 1.0, 0.0).astype(BF)


def div5(v):
    return lax.shift_right_logical(v * 52429, 18)


def remote(src, dst, send, recv, peer):
    return pltpu.make_async_remote_copy(
        src_ref=src, dst_ref=dst, send_sem=send, recv_sem=recv, device_id=peer, device_id_type=MESH
    )


def kernel(
    ent, rel, src_rows, dst_rows, rel_ids, neg_src, neg_dst, count,
    ent_grad, rel_grad,
    ent_here, eb, part, zt, gn, gf, tf, ohs, ohd, ohn, ohf, ohz, ohnt, ohft, ohzt, negs, cnts,
    sf, wf, of, qf, uf, dqf, dpf, dof, dsf, dwf,
    qb, qrow, urow, gmat, gs, dob, ub, sscale, dscale, dwb, dwz,
    dest, dcr, ysend, yrecv, ezs, ezr, rn, rf, rcn, rcf, rn1, rn2, rx1, rx2, ry1, ry2, sn, sx, sy, zsend, zrecv,
    zt_s, zt_r, e_s, e_r, y_s, y_r, m_s, m_r, d_s, d_r, n1_s, n1_r, n2_s, n2_r, f1_s, f1_r, f2_s, f2_r, gn_s, gn_r, gf_s, gf_r,
    dc_s, dc_r, dy_s, dy_r, dz_s, dz_r, rcn_s, rcn_r, rcf_s, rcf_r, rn1_s, rn1_r, rn2_s, rn2_r, rx1_s, rx1_r, rx2_s, rx2_r, ry1_s, ry1_r, ry2_s, ry2_r,
    rz_s, rz_r, in_sem,
):
    dom = lax.axis_index("dom")
    rep = lax.axis_index("rep")
    z = dom // (X * YL)
    x = (dom // YL) % X
    yl = dom % YL
    yh = rep // CORES
    c = rep % CORES
    y = yh * YL + yl
    cm = 1 - c

    def device(dz, dx, dy, core):
        yy = (y + dy) % Y
        return {
            "dom": (((z + dz) % Z) * X + (x + dx) % X) * YL + yy % YL,
            "rep": (yy // YL) * CORES + core,
        }

    def x_at(n):
        return (x + X + n) % X

    def y_at(n):
        return (y + Y + n) % Y

    mate = device(0, 0, 0, cm)
    across = device(0, 0, YL, c)
    far = device(Z // 2, 0, 0, c)

    barrier = pltpu.get_barrier_semaphore()

    @pl.loop(1, Z)
    def _(n):
        pl.semaphore_signal(barrier, inc=1, device_id=device(n, 0, 0, c), device_id_type=MESH)

    for n in range(1, X):
        pl.semaphore_signal(barrier, inc=1, device_id=device(0, n, 0, c), device_id_type=MESH)
    for n in range(1, Y):
        pl.semaphore_signal(barrier, inc=1, device_id=device(0, 0, n, c), device_id_type=MESH)
    pl.semaphore_signal(barrier, inc=1, device_id=mate, device_id_type=MESH)

    read = pltpu.make_async_copy(ent, ent_here, in_sem)
    read.start()

    lane = iota((REL_DEV, 128), 1)
    row5 = iota((REL_DEV, 128), 0)
    for k in range(3):
        tf[k * REL_DEV : (k + 1) * REL_DEV, :] = rel[:, k * 128 : (k + 1) * 128]
    spread16 = one_hot((iota((16, 128), 1) & 15) == iota((16, 128), 0))
    last = nn(rel[:, 384:400].astype(BF), spread16)
    last = jnp.where(lax.shift_right_logical(lane, 4) == row5, last, 0.0)
    tf[15:16, :] = jnp.sum(last, axis=0, keepdims=True)
    zt[0:TILE, :] = tf[...].astype(BF)

    pl.semaphore_wait(barrier, (Z - 1) + (X - 1) + (Y - 1) + 1)

    def slot_device(n):
        return device(jnp.where(n % 2 == 1, (n + 1) // 2, Z - n // 2), 0, 0, c)

    def slot_there(n):
        return jnp.where(n % 2 == 1, jnp.minimum(n + 1, Z - 1), n - 1) if Z > 2 else n

    def tile_of(n):
        return pl.ds(pl.multiple_of(n * TILE, TILE), TILE)

    def tile_copy(n):
        at = slot_there(n)
        return remote(
            zt.at[tile_of(0)], zt.at[tile_of(at)], zt_s.at[n], zt_r.at[at], slot_device(n)
        )

    def tile_arrival(n):
        return remote(zt.at[tile_of(n)], zt.at[tile_of(n)], zt_s.at[n], zt_r.at[n], slot_device(n))

    @pl.loop(NEAR_Z, Z)
    def _(n):
        tile_copy(n).start()

    @pl.loop(1, NEAR_Z)
    def _(n):
        tile_copy(n).start()

    def piece(k):
        at, size, h = PIECES[k]
        return pl.ds(at, size), pl.ds(h * 128, 128)

    def slices(k):
        at, size, h = PIECES[k]
        return slice(at, at + size), slice(h * 128, (h + 1) * 128)

    ent_copies = [
        remote(eb.at[piece(k)], part.at[(rep, *piece(k))], e_s.at[k], e_r.at[k], far)
        for k in range(CHUNKS)
    ]

    read.wait()
    eb[0:D, :] = ent_here[...].astype(BF)
    part[:, D:PAD, :] = jnp.zeros((REP, PAD - D, ROWS), BF)
    eb[D:PAD, :] = jnp.zeros((PAD - D, ROWS), BF)
    qf[D:PAD, :] = jnp.zeros((PAD - D, EDGES), F32)
    uf[D:PAD, :] = jnp.zeros((PAD - D, EDGES), F32)
    dwf[D:PAD, :] = jnp.zeros((PAD - D, EDGES), F32)
    ids = rel_ids[...]
    owner = div5(ids)
    slot = ids - owner * REL_DEV
    owner_z = lax.shift_right_logical(owner, SHIFT_PLANE)
    owner_p = owner & (PI * CORES - 1)
    owner_yh = lax.shift_right_logical(owner_p, SHIFT_CORE) & (YH - 1)
    owner_yl = lax.shift_right_logical(owner_p, SHIFT_YH) & (YL - 1)
    owner_x = lax.shift_right_logical(owner_p, SHIFT_YL)
    block = (((owner_p & (CORES - 1)) * X + owner_x) * YH + owner_yh) * YL + owner_yl
    ring = (owner_z + Z - z) & (Z - 1)
    order = jnp.where(ring * 2 <= Z, jnp.maximum(2 * ring - 1, 0), 2 * (Z - ring))
    row = order * REL_DEV + slot
    pos_n = jnp.where(row < NR, block * NR + row, -1)
    pos_f = jnp.where(row < NR, -1, block * FR + row - NR)
    pos_z = block * Z + order

    ohs[...] = one_hot(iota((ROWS, EDGES), 0) == src_rows[...])
    for b in range(REP):
        ohd[b] = one_hot(iota((ROWS, EDGES), 0) + b * ROWS == dst_rows[...])

    def column(row):
        return jnp.transpose(jnp.broadcast_to(row.astype(F32), (EDGES, EDGES)))[:, :128]

    slot_col = column(slot)
    blocks = PI * CORES
    lanes = iota((EDGES, 128), 1).astype(F32)
    for count_at, at, hot, hot_t in (
        (NR, pos_n, ohn, ohnt),
        (FR, pos_f, ohf, ohft),
        (Z, pos_z, ohz, ohzt),
    ):

        @pl.loop(0, PI)
        def _(n):
            for k in range(CORES):
                hot[k, pl.ds(pl.multiple_of(n * count_at, 16), count_at), :] = one_hot(
                    iota((count_at, EDGES), 0) + (k * PI + n) * count_at == at
                )

        at_col = column(at)
        for t in range(0, blocks * count_at, 128):
            value = one_hot(lanes + float(t) == at_col)
            hot_t[:, t : t + 128] = value[:, : min(128, blocks * count_at - t)]
    slot_mask = lax.shift_right_logical(iota((EDGES, 128), 1), 4).astype(F32) == slot_col

    ones = jnp.ones((16, NEG_PAD), BF)
    negs[...] = jnp.full((2, NEG_PAD), -1, jnp.int32)
    negs[0:1, 0:NEG] = neg_dst[...]
    negs[1:2, 0:NEG] = neg_src[...]
    for b in range(REP):
        cnts[b] = nt(ones, one_hot(iota((ROWS, NEG_PAD), 0) + b * ROWS == negs[0:1, :]))
    cnts[REP] = nt(ones, one_hot(iota((ROWS, NEG_PAD), 0) == negs[1:2, :]))
    sf[...] = nn(eb[0:D, :], ohs[...])

    live = count[...]
    live_row = jnp.where(iota((1, EDGES), 1) < live, 1.0, 0.0)
    live_col = jnp.where(iota((EDGES, ROWS), 0) < live, 1.0 / NEG, 0.0)
    which = lax.shift_right_logical(dst_rows[...], 7) & (HALVES - 1)
    which_col = column(which)
    which_col = jnp.concatenate([which_col, which_col], axis=1)
    for b in range(REP):
        dscale[b] = cnts[b, 0:1, :] * live_col
    for h in range(HALVES):
        sscale[h] = jnp.where(which_col == float(h), cnts[REP, 0:1, :] * live_col, 0.0)

    for k in range(CHUNKS):
        ent_copies[k].start()

    def along_x(n):
        return device(0, n, 0, c)

    def along_y(n):
        return device(0, 0, n, c)

    def same(ref, sends, recvs, n, peer):
        return remote(ref, ref, sends.at[n], recvs.at[n], peer)

    def near_one(n, dx):
        return same(gn.at[c, x_at(dx), y], n1_s, n1_r, n, along_x(n))

    def near_line(n, dy):
        return same(gn.at[c, :, y_at(dy)], n2_s, n2_r, n, along_y(n))

    def far_one(n, dy):
        return same(gf.at[c, x, y_at(dy)], f1_s, f1_r, n, along_y(n))

    def far_line(n, dx):
        return same(gf.at[c, x_at(dx)], f2_s, f2_r, n, along_x(n))

    def near_core(n, core):
        return same(gn.at[core, :, y_at(-n)], gn_s, gn_r, n, mate)

    def far_core(n, core):
        return same(gf.at[core, x_at(-n)], gf_s, gf_r, n, mate)

    def parts_of(k):
        at = lax.shift_right_logical(k, 4)
        s = k & 15
        kind = lax.shift_right_logical(s * 13, 6)
        r = at * REL_DEV + s - kind * REL_DEV
        near = jnp.where((kind < 3) & (r < NR), kind * NR + r, -1)
        distant = jnp.where(r < NR, -1, kind * FR + r - NR)
        return near, jnp.where(kind == 3, 3 * FR + at, distant)

    @pl.loop(1, NEAR_Z)
    def _(n):
        tile_arrival(n).wait_recv()

    shape = (NEAR_ROWS, NEAR_Z * TILE)
    pick = one_hot(iota(shape, 0) == parts_of(iota(shape, 1))[0])
    gn[c, x, y] = nn(pick, zt[0 : NEAR_Z * TILE, :]).astype(BF)
    for n in range(1, X):
        near_one(n, 0).start()

    @pl.loop(NEAR_Z, Z)
    def _(n):
        tile_arrival(n).wait_recv()

    shape = (FAR_ROWS, SLOTS)
    pick = one_hot(iota(shape, 0) == parts_of(iota(shape, 1))[1])
    gf[c, x, y] = nn(pick, zt[...]).astype(BF)
    for n in range(1, Y):
        far_one(n, 0).start()
    for n in range(1, X):
        near_one(n, -n).wait_recv()
    for n in range(1, Y):
        near_line(n, 0).start()
    near_core(0, c).start()
    for n in range(1, Y):
        far_one(n, -n).wait_recv()
    for n in range(1, X):
        far_line(n, 0).start()
    far_core(0, c).start()
    for n in range(1, Y):
        near_line(n, -n).wait_recv()
        near_core(n, c).start()

    at_y = (1 - yh) * CORES + c
    at_mate = yh * CORES + cm
    at_both = (1 - yh) * CORES + cm

    def entity_copy(k, at, sends, recvs, peer):
        ref = part.at[(at, *piece(k))]
        return remote(ref, ref, sends.at[k], recvs.at[k], peer)

    def entity_on(k):
        ent_copies[k].wait_recv()
        entity_copy(k, rep, y_s, y_r, across).start()
        entity_copy(k, rep, m_s, m_r, mate).start()

    def entity_over(k):
        entity_copy(k, at_y, y_s, y_r, across).wait_recv()
        entity_copy(k, at_y, d_s, d_r, mate).start()

    entity_on(0)
    entity_on(1)
    entity_over(0)
    for n in range(1, X):
        far_line(n, -n).wait_recv()
        far_core(n, c).start()
    entity_over(1)
    for n in range(Y):
        near_core(n, cm).wait_recv()
    for n in range(X):
        far_core(n, cm).wait_recv()

    near_table = gn[...].reshape(blocks, NEAR_ROWS, 128)
    far_table = gf[...].reshape(blocks, FAR_ROWS, 128)
    for k in range(3):
        w = nn(ohnt[...], near_table[:, k * NR : (k + 1) * NR, :].reshape(blocks * NR, 128))
        w += nn(ohft[...], far_table[:, k * FR : (k + 1) * FR, :].reshape(blocks * FR, 128))
        wf[k * 128 : (k + 1) * 128, :] = jnp.transpose(w)
    w = nn(ohzt[...], far_table[:, 3 * FR :, :].reshape(blocks * Z, 128))
    fold = one_hot(
        ((iota((128, 128), 0) & 15) == iota((128, 128), 1)) & (iota((128, 128), 0) < 16 * REL_DEV)
    )
    w = nn(jnp.where(slot_mask, w, 0.0).astype(BF), fold)
    wf[384:512, :] = jnp.transpose(w)

    def parts(ref, k):
        re = pl.ds(pl.multiple_of(k * STEP, 8), STEP)
        im = pl.ds(pl.multiple_of(HALF + k * STEP, 8), STEP)
        return ref[re, :], ref[im, :]

    def put(ref, k, re_value, im_value):
        ref[pl.ds(pl.multiple_of(k * STEP, 8), STEP), :] = re_value
        ref[pl.ds(pl.multiple_of(HALF + k * STEP, 8), STEP), :] = im_value

    @pl.loop(0, STEPS)
    def _(k):
        s_re, s_im = parts(sf, k)
        w_re, w_im = parts(wf, k)
        put(qf, k, s_re * w_re - s_im * w_im, s_re * w_im + s_im * w_re)

    qb[...] = qf[0:D, :].astype(BF)
    for k in range(PAD // 128):
        at = slice(k * 128, (k + 1) * 128)
        qrow[:, at] = jnp.transpose(qf[at, :]).astype(BF)

    def half(h):
        lanes = slice(h * 128, (h + 1) * 128)
        for k in range(h * PER_HALF, (h + 1) * PER_HALF):
            entity_copy(k, at_mate, m_s, m_r, mate).wait_recv()
            entity_copy(k, at_both, d_s, d_r, mate).wait_recv()
        total = nn(part[0, 0:D, lanes], ohd[0, lanes, :])
        for b in range(1, REP):
            total += nn(part[b, 0:D, lanes], ohd[b, lanes, :])
        of[...] = total

        def turn(k, positive):
            w_re, w_im = parts(wf, k)
            o_re, o_im = parts(of, k)
            q_re, q_im = parts(qf, k)
            put(uf, k, w_re * o_re + w_im * o_im, w_re * o_im - w_im * o_re)
            return positive + jnp.sum(q_re * o_re + q_im * o_im, axis=0, keepdims=True)

        positive = lax.fori_loop(0, STEPS, turn, jnp.zeros((1, EDGES), F32))
        grad_pos = jnp.where(which == h, -live_row * jax.nn.sigmoid(-positive), 0.0)
        ub[h] = uf[0:D, :].astype(BF)
        for k in range(PAD // 128):
            at = slice(k * 128, (k + 1) * 128)
            urow[:, at] = jnp.transpose(uf[at, :]).astype(BF)
        gs[h] = (jax.nn.sigmoid(nn(urow[...], eb[...])) * sscale[h]).astype(BF)
        for b in range(REP):
            scores = nn(qrow[...], part[b, :, lanes])
            gmat[b, :, lanes] = (jax.nn.sigmoid(scores) * dscale[b, :, lanes]).astype(BF)
        dpf[...] = nt(eb[0:D, :], gs[h])
        total = nt(part[0, 0:D, lanes], gmat[0, :, lanes])
        for b in range(1, REP):
            total += nt(part[b, 0:D, lanes], gmat[b, :, lanes])
        dqf[...] = total

        @pl.loop(0, STEPS)
        def _(k):
            s_re, s_im = parts(sf, k)
            w_re, w_im = parts(wf, k)
            o_re, o_im = parts(of, k)
            q_re, q_im = parts(qf, k)
            u_re, u_im = parts(uf, k)
            dq_re, dq_im = parts(dqf, k)
            dp_re, dp_im = parts(dpf, k)
            dq_re += grad_pos * o_re
            dq_im += grad_pos * o_im
            dp_re += grad_pos * s_re
            dp_im += grad_pos * s_im
            put(
                dof, k,
                grad_pos * q_re + w_re * dp_re - w_im * dp_im,
                grad_pos * q_im + w_re * dp_im + w_im * dp_re,
            )
            dw_re = s_re * dq_re + s_im * dq_im + o_re * dp_re + o_im * dp_im
            dw_im = s_re * dq_im - s_im * dq_re + o_im * dp_re - o_re * dp_im
            ds_re = w_re * dq_re + w_im * dq_im + grad_pos * u_re
            ds_im = w_re * dq_im - w_im * dq_re + grad_pos * u_im
            if h:
                before_re, before_im = parts(dwf, k)
                dw_re += before_re
                dw_im += before_im
                before_re, before_im = parts(dsf, k)
                ds_re += before_re
                ds_im += before_im
            put(dwf, k, dw_re, dw_im)
            put(dsf, k, ds_re, ds_im)

        dob[h] = dof[...].astype(BF)

    def dc_copy(k):
        f, rows = piece(k)
        return remote(dest.at[cm, :, f, rows], dcr.at[:, f, rows], dc_s.at[k], dc_r.at[k], mate)

    def dy_copy(k):
        return remote(ysend.at[piece(k)], yrecv.at[piece(k)], dy_s.at[k], dy_r.at[k], across)

    def dz_copy(k):
        return remote(ezs.at[piece(k)], ezr.at[piece(k)], dz_s.at[k], dz_r.at[k], far)

    def dest_chunk(k):
        f, rows = slices(k)
        h = PIECES[k][2]
        for b in range(REP):
            dest[b % CORES, b // CORES, f, rows] = (
                nn(qb[f, :], gmat[b, :, rows]) + nt(dob[h, f, :], ohd[b, rows, :])
            ).astype(BF)
        dc_copy(k).start()

    def dest_across(k):
        f, rows = slices(k)
        dc_copy(k).wait_recv()
        mine = dest[c, 1 - yh, f, rows].astype(F32) + dcr[1 - yh, f, rows].astype(F32)
        ysend[f, rows] = mine.astype(BF)
        dy_copy(k).start()

    def dest_home(k):
        f, rows = slices(k)
        mine = dest[c, yh, f, rows].astype(F32) + dcr[yh, f, rows].astype(F32)
        dy_copy(k).wait_recv()
        ezs[f, rows] = (mine + yrecv[f, rows].astype(F32)).astype(BF)
        dz_copy(k).start()

    def rel_far(core, n):
        rows = nn(ohf[core, n * Y * FR : (n + 1) * Y * FR, :], dwb[...]).astype(BF)
        ends = nn(ohz[core, n * Y * Z : (n + 1) * Y * Z, :], dwz[...]).astype(BF)
        for m in range(Y):
            for k in range(3):
                rf[core, n, m, k * FR : (k + 1) * FR, :] = rows[
                    m * FR : (m + 1) * FR, k * 128 : (k + 1) * 128
                ]
            rf[core, n, m, 3 * FR :, :] = ends[m * Z : (m + 1) * Z, :]

    def rel_near(core, n):
        rows = nn(ohn[core, n * Y * NR : (n + 1) * Y * NR, :], dwb[...]).astype(BF)
        for m in range(Y):
            for k in range(3):
                rn[core, n, m, k * NR : (k + 1) * NR, :] = rows[
                    m * NR : (m + 1) * NR, k * 128 : (k + 1) * 128
                ]

    def rc_near(n):
        return remote(rn.at[cm, n], rcn.at[n], rcn_s.at[n], rcn_r.at[n], mate)

    def rc_far(n):
        return remote(rf.at[cm, n], rcf.at[n], rcf_s.at[n], rcf_r.at[n], mate)

    def x_first(n):
        ref = rf.at[c, x_at(n), :, 0:FH]
        return remote(ref, rx1.at[n], rx1_s.at[n], rx1_r.at[n], along_x(n))

    def x_second(n):
        return remote(sx.at[y_at(n)], rx2.at[n], rx2_s.at[n], rx2_r.at[n], along_y(n))

    def y_first(n):
        ref = rf.at[c, :, y_at(n), FH:FAR_ROWS]
        return remote(ref, ry1.at[n], ry1_s.at[n], ry1_r.at[n], along_y(n))

    def y_second(n):
        return remote(sy.at[x_at(n)], ry2.at[n], ry2_s.at[n], ry2_r.at[n], along_x(n))

    def near_first(n):
        return remote(rn.at[c, :, y_at(n)], rn1.at[n], rn1_s.at[n], rn1_r.at[n], along_y(n))

    def near_second(n):
        return remote(sn.at[x_at(n)], rn2.at[n], rn2_s.at[n], rn2_r.at[n], along_x(n))

    def far_to_plane():
        for n in range(X):
            rc_far(n).wait_recv()
        for n in [*range(1, X), 0]:
            at = x_at(n)
            rf[c, at] = (rf[c, at].astype(F32) + rcf[at].astype(F32)).astype(BF)
            if n:
                x_first(n).start()
        for n in range(1, Y):
            y_first(n).start()

    def near_to_y():
        for n in range(X):
            rc_near(n).wait_recv()
        for n in [*range(1, Y), 0]:
            at = y_at(n)
            rn[c, :, at] = (rn[c, :, at].astype(F32) + rcn[:, at].astype(F32)).astype(BF)
            if n:
                near_first(n).start()

    def far_turn():
        for n in range(1, X):
            x_first(n).wait_recv()
        for n in [*range(1, Y), 0]:
            at = y_at(n)
            total = rf[c, x, at, 0:FH, :].astype(F32)
            for m in range(1, X):
                total += rx1[m, at].astype(F32)
            sx[at] = total.astype(BF)
            if n:
                x_second(n).start()
        for n in range(1, Y):
            y_first(n).wait_recv()
        for n in [*range(1, X), 0]:
            at = x_at(n)
            total = rf[c, at, y, FH:FAR_ROWS, :].astype(F32)
            for m in range(1, Y):
                total += ry1[m, at].astype(F32)
            sy[at] = total.astype(BF)
            if n:
                y_second(n).start()

    def near_to_x():
        for n in range(1, Y):
            near_first(n).wait_recv()
        for n in [*range(1, X), 0]:
            at = x_at(n)
            total = rn[c, at, y].astype(F32)
            for m in range(1, Y):
                total += rn1[m, at].astype(F32)
            sn[at] = total.astype(BF)
            if n:
                near_second(n).start()

    def rz_copy(n):
        at = slot_there(n)
        return remote(zsend.at[tile_of(n)], zrecv.at[at], rz_s.at[n], rz_r.at[at], slot_device(n))

    def rz_arrival(n):
        return remote(zsend.at[tile_of(n)], zrecv.at[n], rz_s.at[n], rz_r.at[n], slot_device(n))

    half(0)
    dest_chunk(0)
    dest_chunk(1)
    entity_on(2)
    dest_across(0)
    dest_across(1)
    entity_on(3)
    entity_over(2)
    dest_home(0)
    dest_home(1)
    entity_over(3)
    half(1)
    for k in range(3):
        dwb[:, k * 128 : (k + 1) * 128] = jnp.transpose(dwf[k * 128 : (k + 1) * 128, :]).astype(BF)
    spread = one_hot(
        ((iota((128, 128), 1) & 15) == iota((128, 128), 0)) & (iota((128, 128), 1) < 16 * REL_DEV)
    )
    tail = nn(jnp.transpose(dwf[384:512, :]).astype(BF), spread)
    dwz[...] = jnp.where(slot_mask, tail, 0.0).astype(BF)
    for n in range(X):
        rel_far(cm, n)
        rc_far(n).start()
    dest_chunk(2)
    dest_chunk(3)
    for n in range(X):
        rel_near(cm, n)
        rc_near(n).start()
    for n in range(X):
        rel_far(c, n)
    far_to_plane()
    dest_across(2)
    dest_across(3)
    for n in range(X):
        rel_near(c, n)
    near_to_y()
    dest_home(2)
    dest_home(3)
    far_turn()
    near_to_x()

    ds_hi = dsf[...].astype(BF)
    ds_lo = (dsf[...] - ds_hi.astype(F32)).astype(BF)
    total = nt(ds_hi, ohs[...]) + nt(ds_lo, ohs[...])
    for h in range(HALVES):
        total += nn(ub[h], gs[h])
    sf[...] = total

    total = sx[y].astype(F32)
    for n in range(1, Y):
        x_second(n).wait_recv()
        total += rx2[n].astype(F32)
    other = sy[x].astype(F32)
    for n in range(1, X):
        y_second(n).wait_recv()
        other += ry2[n].astype(F32)
    far_sum = jnp.concatenate([total, other], axis=0).astype(BF)
    shape = (SLOTS, FAR_ROWS)
    pick = one_hot(iota(shape, 1) == parts_of(iota(shape, 0))[1])
    tiles = nn(pick, far_sum)
    zsend[NEAR_Z * TILE :, :] = tiles[NEAR_Z * TILE :, :].astype(BF)

    @pl.loop(NEAR_Z, Z)
    def _(n):
        rz_copy(n).start()

    total = sn[x].astype(F32)
    for n in range(1, X):
        near_second(n).wait_recv()
        total += rn2[n].astype(F32)
    near_sum = total.astype(BF)
    shape = (NEAR_Z * TILE, NEAR_ROWS)
    pick = one_hot(iota(shape, 1) == parts_of(iota(shape, 0))[0])
    zsend[0 : NEAR_Z * TILE, :] = (nn(pick, near_sum) + tiles[0 : NEAR_Z * TILE, :]).astype(BF)

    @pl.loop(1, NEAR_Z)
    def _(n):
        rz_copy(n).start()

    for k in range(CHUNKS):
        dz_copy(k).wait_recv()
    ent_grad[...] = sf[...] + ezr[...].astype(F32)

    def add_tile(n, acc):
        rz_arrival(n).wait_recv()
        return acc + zrecv[n].astype(F32)

    rel_grad[...] = lax.fori_loop(1, Z, add_tile, zsend[0:TILE, :].astype(F32))

    for k in range(CHUNKS):
        ent_copies[k].wait_send()
        entity_copy(k, rep, y_s, y_r, across).wait_send()
        entity_copy(k, rep, m_s, m_r, mate).wait_send()
        entity_copy(k, at_y, d_s, d_r, mate).wait_send()
        dc_copy(k).wait_send()
        dy_copy(k).wait_send()
        dz_copy(k).wait_send()
    for n in range(X):
        rc_near(n).wait_send()
        rc_far(n).wait_send()
        far_core(n, c).wait_send()
    for n in range(Y):
        near_core(n, c).wait_send()
    for n in range(1, X):
        near_one(n, 0).wait_send()
        far_line(n, 0).wait_send()
        x_first(n).wait_send()
        y_second(n).wait_send()
        near_second(n).wait_send()
    for n in range(1, Y):
        near_line(n, 0).wait_send()
        far_one(n, 0).wait_send()
        x_second(n).wait_send()
        y_first(n).wait_send()
        near_first(n).wait_send()

    @pl.loop(1, Z)
    def _(n):
        tile_copy(n).wait_send()
        rz_copy(n).wait_send()


def update(
    ent, state, rel, rel_state, ent_grad, rel_grad, new_ent, new_state, new_rel, new_rel_state
):
    grad = ent_grad[...]
    fresh = state[...] + jnp.sum(grad * grad, axis=0, keepdims=True) * (1.0 / D)
    new_state[...] = fresh
    new_ent[...] = ent[...] - grad * (0.5 / jnp.sqrt(fresh))

    lane = iota((REL_DEV, 128), 1)
    row5 = iota((REL_DEV, 128), 0)
    own_slot = lax.shift_right_logical(lane, 4) == row5
    ends = jnp.where(own_slot, jnp.broadcast_to(rel_grad[15:16, :], (REL_DEV, 128)), 0.0)
    fold_f = jnp.where(
        ((iota((128, 128), 0) & 15) == iota((128, 128), 1)) & (iota((128, 128), 0) < 16 * REL_DEV),
        1.0,
        0.0,
    )
    ends = jnp.dot(ends, fold_f, precision=lax.Precision.HIGHEST, preferred_element_type=F32)
    pieces = [rel_grad[k * REL_DEV : (k + 1) * REL_DEV, :] for k in range(3)] + [ends]
    squares = jnp.sum(sum(piece * piece for piece in pieces), axis=1, keepdims=True)
    eye = iota((REL_DEV, REL_DEV), 0) == iota((REL_DEV, REL_DEV), 1)
    old = jnp.broadcast_to(rel_state[...], (REL_DEV, REL_DEV))
    old = jnp.sum(jnp.where(eye, old, 0.0), axis=1, keepdims=True)
    fresh = old + squares * (1.0 / D)
    new_rel_state[...] = jnp.sum(
        jnp.where(eye, jnp.broadcast_to(fresh, (REL_DEV, REL_DEV)), 0.0), axis=0, keepdims=True
    )
    scale = 0.5 / jnp.sqrt(fresh)
    for k in range(3):
        at = slice(k * 128, (k + 1) * 128)
        new_rel[:, at] = rel[:, at] - pieces[k] * scale
    new_rel[:, 384:400] = rel[:, 384:400] - ends[:, 0:16] * scale


def scratch():
    vm = pltpu.VMEM
    dma = pltpu.SemaphoreType.DMA
    blocks = PI * CORES
    return [
        vm((D, ROWS), F32),
        vm((PAD, ROWS), BF),
        vm((REP, PAD, ROWS), BF),
        vm((SLOTS, 128), BF),
        vm((CORES, X, Y, NEAR_ROWS, 128), BF),
        vm((CORES, X, Y, FAR_ROWS, 128), BF),
        vm((TILE, 128), F32),
        vm((ROWS, EDGES), BF),
        vm((REP, ROWS, EDGES), BF),
        vm((CORES, PI * NR, EDGES), BF),
        vm((CORES, PI * FR, EDGES), BF),
        vm((CORES, PI * Z, EDGES), BF),
        vm((EDGES, blocks * NR), BF),
        vm((EDGES, blocks * FR), BF),
        vm((EDGES, blocks * Z), BF),
        vm((2, NEG_PAD), jnp.int32),
        vm((REP + 1, 16, ROWS), F32),
        vm((D, EDGES), F32),
        vm((PAD, EDGES), F32),
        vm((D, EDGES), F32),
        vm((PAD, EDGES), F32),
        vm((PAD, EDGES), F32),
        vm((D, EDGES), F32),
        vm((D, EDGES), F32),
        vm((D, EDGES), F32),
        vm((D, EDGES), F32),
        vm((PAD, EDGES), F32),
        vm((D, EDGES), BF),
        vm((EDGES, PAD), BF),
        vm((EDGES, PAD), BF),
        vm((REP, EDGES, ROWS), BF),
        vm((HALVES, EDGES, ROWS), BF),
        vm((HALVES, D, EDGES), BF),
        vm((HALVES, D, EDGES), BF),
        vm((HALVES, EDGES, ROWS), F32),
        vm((REP, EDGES, ROWS), F32),
        vm((EDGES, 384), BF),
        vm((EDGES, 128), BF),
        vm((CORES, YH, D, ROWS), BF),
        vm((YH, D, ROWS), BF),
        vm((D, ROWS), BF),
        vm((D, ROWS), BF),
        vm((D, ROWS), BF),
        vm((D, ROWS), BF),
        vm((CORES, X, Y, NEAR_ROWS, 128), BF),
        vm((CORES, X, Y, FAR_ROWS, 128), BF),
        vm((X, Y, NEAR_ROWS, 128), BF),
        vm((X, Y, FAR_ROWS, 128), BF),
        vm((Y, X, NEAR_ROWS, 128), BF),
        vm((X, NEAR_ROWS, 128), BF),
        vm((X, Y, FH, 128), BF),
        vm((Y, FH, 128), BF),
        vm((Y, X, FH, 128), BF),
        vm((X, FH, 128), BF),
        vm((X, NEAR_ROWS, 128), BF),
        vm((Y, FH, 128), BF),
        vm((X, FH, 128), BF),
        vm((SLOTS, 128), BF),
        vm((Z, TILE, 128), BF),
    ] + [
        dma((n,))
        for n in [Z] * 2 + [CHUNKS] * 8 + [max(X, Y)] * 12 + [CHUNKS] * 6 + [max(X, Y)] * 16 + [Z] * 2
    ] + [dma]


def local(
    entities, ent_state, relations, rel_state, src_rows, dst_rows, rel_ids, neg_src, neg_dst, edge_count
):
    vmem = pl.BlockSpec(memory_space=pltpu.VMEM)
    ent = entities.T
    ent_grad, rel_grad = pl.pallas_call(
        kernel,
        out_shape=(
            jax.ShapeDtypeStruct((D, ROWS), F32),
            jax.ShapeDtypeStruct((TILE, 128), F32),
        ),
        in_specs=[pl.BlockSpec(memory_space=pl.ANY)] + [vmem] * 7,
        out_specs=(vmem,) * 2,
        scratch_shapes=scratch(),
        compiler_params=pltpu.CompilerParams(
            collective_id=0, has_side_effects=True, vmem_limit_bytes=56 * 1024 * 1024
        ),
        name="bucket_round",
    )(
        ent, relations, src_rows, dst_rows, rel_ids, neg_src, neg_dst, edge_count.reshape(1, 1)
    )
    new_ent, new_state, new_rel, new_rel_state = pl.pallas_call(
        update,
        out_shape=(
            jax.ShapeDtypeStruct((D, ROWS), F32),
            jax.ShapeDtypeStruct((1, ROWS), F32),
            jax.ShapeDtypeStruct((REL_DEV, D), F32),
            jax.ShapeDtypeStruct((1, REL_DEV), F32),
        ),
        in_specs=[vmem] * 6,
        out_specs=(vmem,) * 4,
        name="row_update",
    )(
        ent,
        ent_state.reshape(1, ROWS),
        relations,
        rel_state.reshape(1, REL_DEV),
        ent_grad,
        rel_grad,
    )
    return (new_ent.T, new_state.reshape(ROWS), new_rel, new_rel_state.reshape(REL_DEV))


def solution(mesh):
    rows = P(("dom", "rep"), None)
    flat = P(("dom", "rep"))
    return jax.shard_map(
        local,
        mesh=mesh,
        in_specs=(rows, flat, rows, flat, rows, rows, rows, rows, rows, flat),
        out_specs=(rows, flat, rows, flat),
        check_vma=False,
    )
```

time: 93.7 us -> 90.4 us (0.965)
  local copies, waits for them, and re-layouts: 3.5 us -> 0 us
    unnamed x10 -> x0, local copies, waits for them, and re-layouts: 3.5 us -> none
    pallas_call x0 -> x1, Pallas kernels: none -> 2.17 us  [local(): pl.pallas_call(update, out_shape=(jax.ShapeDtypeStruct((D, ROWS), F32), j...]
    pallas_call x1, Pallas kernels: 87.2 us -> 85.9 us  [local(): pl.pallas_call(kernel, out_shape=(jax.ShapeDtypeStruct((D, ROWS), F32), j...]
where the time goes in v2:
time: 90.4 us; the launch traced here: 89.4 us
  Pallas kernels  88.1 us (97%)
  between operations  1.29 us (1%)
    pallas_call x1, Pallas kernels, local(): pl.pallas_call(kernel, out_shape=(jax.ShapeDtypeStruct((D, ROWS), F32), j...  85.9 us
    pallas_call x1, Pallas kernels, local(): pl.pallas_call(update, out_shape=(jax.ShapeDtypeStruct((D, ROWS), F32), j...  2.17 us

profile of v2, /device:TPU:6, one launch (start us, length us, event | category | flops | bytes accessed | tf_op | source)
XLA Modules:
  0.0 89.4 jit_solution(8432693203406702996)
XLA Ops:
  1.3 85.9 %bucket_round.1 = (f32[400,256]{1,0:T(8,128)}, f32[16,128]{1,0:T(8,128)}) custom-call(f32[400,256]{1,0:T(8,128)} %bitcast.8, f32[5,400]{1,0:T(8,128)} %rel.3, s32[1,256]{1,0:T(1,128)} %src_rows.1, s32[1,256]{1,0:T(1,128)} %dst_rows.1, s32[1,256]{1,0:T(1,128)} %rel_ids.1, s32[1,1000]{1,0:T(1,128)} %neg_src.1, s32[1,1000]{1,0:T(1,128)} %neg_dst.1, ...), custom_call_target="tpu_custom_call" | custom-call | tf_op jit(solution)/shard_map/bucket_round/pallas_call | solution.py:816
  87.2 2.2 %row_update.1 = (f32[400,256]{1,0:T(8,128)}, f32[1,256]{1,0:T(1,128)}, f32[5,400]{1,0:T(8,128)}, f32[1,5]{1,0:T(1,128)}) custom-call(f32[400,256]{1,0:T(8,128)} %bitcast.9, f32[1,256]{1,0:T(1,128)} %bitcast.10, f32[5,400]{1,0:T(8,128)} %rel.3, f32[1,5]{1,0:T(1,128)} %bitcast.11, f32[400,256]{1,0:T(8,128)} %get-tuple-element.10.ent_grad, ...), custom_call_target="tpu_custom_call" | custom-call | tf_op jit(solution)/shard_map/row_update/pallas_call | solution.py:832

commit v3 on v2

--- a/solution.py
+++ b/solution.py
@@ -69,9 +69,9 @@
 
 
 def kernel(
-    ent, rel, src_rows, dst_rows, rel_ids, neg_src, neg_dst, count,
+    ent, rel_in, src_in, dst_in, ids_in, neg_src_in, neg_dst_in, count,
     ent_grad, rel_grad,
-    ent_here, eb, part, zt, gn, gf, tf, ohs, ohd, ohn, ohf, ohz, ohnt, ohft, ohzt, negs, cnts,
+    ent_here, rel, src_rows, dst_rows, rel_ids, neg_src, neg_dst, eb, part, zt, gn, gf, tf, ohs, ohd, ohn, ohf, ohz, ohnt, ohft, ohzt, negs, cnts,
     sf, wf, of, qf, uf, dqf, dpf, dof, dsf, dwf,
     qb, qrow, urow, gmat, gs, dob, ub, sscale, dscale, dwb, dwz,
     dest, dcr, ysend, yrecv, ezs, ezr, rn, rf, rcn, rcf, rn1, rn2, rx1, rx2, ry1, ry2, sn, sx, sy, zsend, zrecv,
@@ -106,6 +106,21 @@
     across = device(0, 0, YL, c)
     far = device(Z // 2, 0, 0, c)
 
+    reads = [
+        pltpu.make_async_copy(source, here, in_sem.at[n])
+        for n, (source, here) in enumerate(
+            (
+                (rel_in, rel),
+                (ent, ent_here),
+                (src_in, src_rows),
+                (dst_in, dst_rows),
+                (ids_in, rel_ids),
+                (neg_src_in, neg_src),
+                (neg_dst_in, neg_dst),
+            )
+        )
+    ]
+
     barrier = pltpu.get_barrier_semaphore()
 
     @pl.loop(1, Z)
@@ -118,9 +133,10 @@
         pl.semaphore_signal(barrier, inc=1, device_id=device(0, 0, n, c), device_id_type=MESH)
     pl.semaphore_signal(barrier, inc=1, device_id=mate, device_id_type=MESH)
 
-    read = pltpu.make_async_copy(ent, ent_here, in_sem)
-    read.start()
-
+    for read in reads:
+        read.start()
+
+    reads[0].wait()
     lane = iota((REL_DEV, 128), 1)
     row5 = iota((REL_DEV, 128), 0)
     for k in range(3):
@@ -172,7 +188,8 @@
         for k in range(CHUNKS)
     ]
 
-    read.wait()
+    for read in reads[1:]:
+        read.wait()
     eb[0:D, :] = ent_here[...].astype(BF)
     part[:, D:PAD, :] = jnp.zeros((REP, PAD - D, ROWS), BF)
     eb[D:PAD, :] = jnp.zeros((PAD - D, ROWS), BF)
@@ -269,7 +286,7 @@
         return same(gf.at[c, x_at(dx)], f2_s, f2_r, n, along_x(n))
 
     def near_core(n, core):
-        return same(gn.at[core, :, y_at(-n)], gn_s, gn_r, n, mate)
+        return same(gn.at[core], gn_s, gn_r, n, mate)
 
     def far_core(n, core):
         return same(gf.at[core, x_at(-n)], gf_s, gf_r, n, mate)
@@ -306,7 +323,6 @@
         near_one(n, -n).wait_recv()
     for n in range(1, Y):
         near_line(n, 0).start()
-    near_core(0, c).start()
     for n in range(1, Y):
         far_one(n, -n).wait_recv()
     for n in range(1, X):
@@ -314,7 +330,7 @@
     far_core(0, c).start()
     for n in range(1, Y):
         near_line(n, -n).wait_recv()
-        near_core(n, c).start()
+    near_core(0, c).start()
 
     at_y = (1 - yh) * CORES + c
     at_mate = yh * CORES + cm
@@ -340,8 +356,8 @@
         far_line(n, -n).wait_recv()
         far_core(n, c).start()
     entity_over(1)
-    for n in range(Y):
-        near_core(n, cm).wait_recv()
+    entity_on(2)
+    near_core(0, cm).wait_recv()
     for n in range(X):
         far_core(n, cm).wait_recv()
 
@@ -497,7 +513,7 @@
                 ]
 
     def rc_near(n):
-        return remote(rn.at[cm, n], rcn.at[n], rcn_s.at[n], rcn_r.at[n], mate)
+        return remote(rn.at[cm], rcn, rcn_s.at[n], rcn_r.at[n], mate)
 
     def rc_far(n):
         return remote(rf.at[cm, n], rcf.at[n], rcf_s.at[n], rcf_r.at[n], mate)
@@ -534,8 +550,7 @@
             y_first(n).start()
 
     def near_to_y():
-        for n in range(X):
-            rc_near(n).wait_recv()
+        rc_near(0).wait_recv()
         for n in [*range(1, Y), 0]:
             at = y_at(n)
             rn[c, :, at] = (rn[c, :, at].astype(F32) + rcn[:, at].astype(F32)).astype(BF)
@@ -586,15 +601,16 @@
     half(0)
     dest_chunk(0)
     dest_chunk(1)
-    entity_on(2)
+    entity_over(2)
     dest_across(0)
     dest_across(1)
     entity_on(3)
-    entity_over(2)
     dest_home(0)
     dest_home(1)
     entity_over(3)
     half(1)
+    dest_chunk(2)
+    dest_chunk(3)
     for k in range(3):
         dwb[:, k * 128 : (k + 1) * 128] = jnp.transpose(dwf[k * 128 : (k + 1) * 128, :]).astype(BF)
     spread = one_hot(
@@ -605,11 +621,9 @@
     for n in range(X):
         rel_far(cm, n)
         rc_far(n).start()
-    dest_chunk(2)
-    dest_chunk(3)
     for n in range(X):
         rel_near(cm, n)
-        rc_near(n).start()
+    rc_near(0).start()
     for n in range(X):
         rel_far(c, n)
     far_to_plane()
@@ -620,6 +634,25 @@
     near_to_y()
     dest_home(2)
     dest_home(3)
+    for k in range(CHUNKS):
+        ent_copies[k].wait_send()
+        entity_copy(k, rep, y_s, y_r, across).wait_send()
+        entity_copy(k, rep, m_s, m_r, mate).wait_send()
+        entity_copy(k, at_y, d_s, d_r, mate).wait_send()
+    for n in range(X):
+        far_core(n, c).wait_send()
+    near_core(0, c).wait_send()
+    for n in range(1, X):
+        near_one(n, 0).wait_send()
+        far_line(n, 0).wait_send()
+    for n in range(1, Y):
+        near_line(n, 0).wait_send()
+        far_one(n, 0).wait_send()
+
+    @pl.loop(1, Z)
+    def _(n):
+        tile_copy(n).wait_send()
+
     far_turn()
     near_to_x()
 
@@ -629,6 +662,17 @@
     for h in range(HALVES):
         total += nn(ub[h], gs[h])
     sf[...] = total
+    for k in range(CHUNKS):
+        dc_copy(k).wait_send()
+        dy_copy(k).wait_send()
+    for n in range(X):
+        rc_far(n).wait_send()
+    rc_near(0).wait_send()
+    for n in range(1, X):
+        x_first(n).wait_send()
+    for n in range(1, Y):
+        y_first(n).wait_send()
+        near_first(n).wait_send()
 
     total = sx[y].astype(F32)
     for n in range(1, Y):
@@ -661,6 +705,18 @@
     def _(n):
         rz_copy(n).start()
 
+    for n in range(1, X):
+        y_second(n).wait_send()
+        near_second(n).wait_send()
+    for n in range(1, Y):
+        x_second(n).wait_send()
+    for k in range(CHUNKS):
+        dz_copy(k).wait_send()
+
+    @pl.loop(1, Z)
+    def _(n):
+        rz_copy(n).wait_send()
+
     for k in range(CHUNKS):
         dz_copy(k).wait_recv()
     ent_grad[...] = sf[...] + ezr[...].astype(F32)
@@ -670,38 +726,6 @@
         return acc + zrecv[n].astype(F32)
 
     rel_grad[...] = lax.fori_loop(1, Z, add_tile, zsend[0:TILE, :].astype(F32))
-
-    for k in range(CHUNKS):
-        ent_copies[k].wait_send()
-        entity_copy(k, rep, y_s, y_r, across).wait_send()
-        entity_copy(k, rep, m_s, m_r, mate).wait_send()
-        entity_copy(k, at_y, d_s, d_r, mate).wait_send()
-        dc_copy(k).wait_send()
-        dy_copy(k).wait_send()
-        dz_copy(k).wait_send()
-    for n in range(X):
-        rc_near(n).wait_send()
-        rc_far(n).wait_send()
-        far_core(n, c).wait_send()
-    for n in range(Y):
-        near_core(n, c).wait_send()
-    for n in range(1, X):
-        near_one(n, 0).wait_send()
-        far_line(n, 0).wait_send()
-        x_first(n).wait_send()
-        y_second(n).wait_send()
-        near_second(n).wait_send()
-    for n in range(1, Y):
-        near_line(n, 0).wait_send()
-        far_one(n, 0).wait_send()
-        x_second(n).wait_send()
-        y_first(n).wait_send()
-        near_first(n).wait_send()
-
-    @pl.loop(1, Z)
-    def _(n):
-        tile_copy(n).wait_send()
-        rz_copy(n).wait_send()
 
 
 def update(
@@ -744,6 +768,12 @@
     blocks = PI * CORES
     return [
         vm((D, ROWS), F32),
+        vm((REL_DEV, D), F32),
+        vm((1, EDGES), jnp.int32),
+        vm((1, EDGES), jnp.int32),
+        vm((1, EDGES), jnp.int32),
+        vm((1, NEG), jnp.int32),
+        vm((1, NEG), jnp.int32),
         vm((PAD, ROWS), BF),
         vm((REP, PAD, ROWS), BF),
         vm((SLOTS, 128), BF),
@@ -805,7 +835,7 @@
     ] + [
         dma((n,))
         for n in [Z] * 2 + [CHUNKS] * 8 + [max(X, Y)] * 12 + [CHUNKS] * 6 + [max(X, Y)] * 16 + [Z] * 2
-    ] + [dma]
+    ] + [dma((7,))]
 
 
 def local(
@@ -819,7 +849,7 @@
             jax.ShapeDtypeStruct((D, ROWS), F32),
             jax.ShapeDtypeStruct((TILE, 128), F32),
         ),
-        in_specs=[pl.BlockSpec(memory_space=pl.ANY)] + [vmem] * 7,
+        in_specs=[pl.BlockSpec(memory_space=pl.ANY)] * 7 + [vmem],
         out_specs=(vmem,) * 2,
         scratch_shapes=scratch(),
         compiler_params=pltpu.CompilerParams(

time: 90.4 us -> 87.8 us (0.971)
  Pallas kernels: 88.1 us -> 86.3 us
    pallas_call x1, Pallas kernels: 85.9 us -> 84.2 us  [local(): pl.pallas_call(kernel, out_shape=(jax.ShapeDtypeStruct((D, ROWS), F32), j...]
where the time goes in v3:
time: 87.8 us; the launch traced here: 87.6 us
  Pallas kernels  86.3 us (98%)
  between operations  1.29 us (1%)
    pallas_call x1, Pallas kernels, local(): pl.pallas_call(kernel, out_shape=(jax.ShapeDtypeStruct((D, ROWS), F32), j...  84.2 us
    pallas_call x1, Pallas kernels, local(): pl.pallas_call(update, out_shape=(jax.ShapeDtypeStruct((D, ROWS), F32), j...  2.17 us

profile of v3, /device:TPU:6, one launch (start us, length us, event | category | flops | bytes accessed | tf_op | source)
XLA Modules:
  0.0 87.6 jit_solution(5278938817494781100)
XLA Ops:
  1.3 84.2 %bucket_round.1 = (f32[400,256]{1,0:T(8,128)}, f32[16,128]{1,0:T(8,128)}) custom-call(f32[400,256]{1,0:T(8,128)} %bitcast.8, f32[5,400]{1,0:T(8,128)} %rel.1, s32[1,256]{1,0:T(1,128)} %src_in.1, s32[1,256]{1,0:T(1,128)} %dst_in.1, s32[1,256]{1,0:T(1,128)} %ids_in.1, s32[1,1000]{1,0:T(1,128)} %neg_src_in.1, s32[1,1000]{1,0:T(1,128)} %neg_dst_in.1, ...), custom_call_target="tpu_custom_call" | custom-call | tf_op jit(solution)/shard_map/bucket_round/pallas_call | solution.py:846
  85.5 2.2 %row_update.1 = (f32[400,256]{1,0:T(8,128)}, f32[1,256]{1,0:T(1,128)}, f32[5,400]{1,0:T(8,128)}, f32[1,5]{1,0:T(1,128)}) custom-call(f32[400,256]{1,0:T(8,128)} %bitcast.9, f32[1,256]{1,0:T(1,128)} %bitcast.10, f32[5,400]{1,0:T(8,128)} %rel.1, f32[1,5]{1,0:T(1,128)} %bitcast.11, f32[400,256]{1,0:T(8,128)} %get-tuple-element.10.ent_grad, ...), custom_call_target="tpu_custom_call" | custom-call | tf_op jit(solution)/shard_map/row_update/pallas_call | solution.py:862

commit v4 on v3

--- a/solution.py
+++ b/solution.py
@@ -28,9 +28,8 @@
 FH = FAR_ROWS // 2
 HALVES = ROWS // 128
 SPLIT = 208
-PIECES = [(at, size, h) for h in range(HALVES) for at, size in ((0, SPLIT), (SPLIT, D - SPLIT))]
+PIECES = [(0, D, 0), (0, SPLIT, 1), (SPLIT, D - SPLIT, 1)]
 CHUNKS = len(PIECES)
-PER_HALF = CHUNKS // HALVES
 STEP = 40
 STEPS = HALF // STEP
 SHIFT_PLANE = (PI * CORES).bit_length() - 1
@@ -350,13 +349,11 @@
         entity_copy(k, at_y, d_s, d_r, mate).start()
 
     entity_on(0)
-    entity_on(1)
     entity_over(0)
     for n in range(1, X):
         far_line(n, -n).wait_recv()
         far_core(n, c).start()
-    entity_over(1)
-    entity_on(2)
+    entity_on(1)
     near_core(0, cm).wait_recv()
     for n in range(X):
         far_core(n, cm).wait_recv()
@@ -396,7 +393,7 @@
 
     def half(h):
         lanes = slice(h * 128, (h + 1) * 128)
-        for k in range(h * PER_HALF, (h + 1) * PER_HALF):
+        for k in (k for k in range(CHUNKS) if PIECES[k][2] == h):
             entity_copy(k, at_mate, m_s, m_r, mate).wait_recv()
             entity_copy(k, at_both, d_s, d_r, mate).wait_recv()
         total = nn(part[0, 0:D, lanes], ohd[0, lanes, :])
@@ -600,17 +597,14 @@
 
     half(0)
     dest_chunk(0)
+    entity_over(1)
+    dest_across(0)
+    entity_on(2)
+    dest_home(0)
+    entity_over(2)
+    half(1)
     dest_chunk(1)
-    entity_over(2)
-    dest_across(0)
-    dest_across(1)
-    entity_on(3)
-    dest_home(0)
-    dest_home(1)
-    entity_over(3)
-    half(1)
     dest_chunk(2)
-    dest_chunk(3)
     for k in range(3):
         dwb[:, k * 128 : (k + 1) * 128] = jnp.transpose(dwf[k * 128 : (k + 1) * 128, :]).astype(BF)
     spread = one_hot(
@@ -627,13 +621,13 @@
     for n in range(X):
         rel_far(c, n)
     far_to_plane()
+    dest_across(1)
     dest_across(2)
-    dest_across(3)
     for n in range(X):
         rel_near(c, n)
     near_to_y()
+    dest_home(1)
     dest_home(2)
-    dest_home(3)
     for k in range(CHUNKS):
         ent_copies[k].wait_send()
         entity_copy(k, rep, y_s, y_r, across).wait_send()

time: 87.8 us -> 89.9 us (1.024); the launches traced: 87.6 us -> 88.7 us
  Pallas kernels: 86.3 us -> 87.4 us
    pallas_call x1, Pallas kernels: 84.2 us -> 85.3 us  [local(): pl.pallas_call(kernel, out_shape=(jax.ShapeDtypeStruct((D, ROWS), F32), j...]
where the time goes in v4:
time: 89.9 us; the launch traced here: 88.7 us
  Pallas kernels  87.4 us (97%)
  between operations  1.29 us (1%)
    pallas_call x1, Pallas kernels, local(): pl.pallas_call(kernel, out_shape=(jax.ShapeDtypeStruct((D, ROWS), F32), j...  85.3 us
    pallas_call x1, Pallas kernels, local(): pl.pallas_call(update, out_shape=(jax.ShapeDtypeStruct((D, ROWS), F32), j...  2.17 us

profile of v4, /device:TPU:6, one launch (start us, length us, event | category | flops | bytes accessed | tf_op | source)
XLA Modules:
  0.0 88.7 jit_solution(3771707210811998241)
XLA Ops:
  1.3 85.3 %bucket_round.1 = (f32[400,256]{1,0:T(8,128)}, f32[16,128]{1,0:T(8,128)}) custom-call(f32[400,256]{1,0:T(8,128)} %bitcast.8, f32[5,400]{1,0:T(8,128)} %rel.1, s32[1,256]{1,0:T(1,128)} %src_in.1, s32[1,256]{1,0:T(1,128)} %dst_in.1, s32[1,256]{1,0:T(1,128)} %ids_in.1, s32[1,1000]{1,0:T(1,128)} %neg_src_in.1, s32[1,1000]{1,0:T(1,128)} %neg_dst_in.1, ...), custom_call_target="tpu_custom_call" | custom-call | tf_op jit(solution)/shard_map/bucket_round/pallas_call | solution.py:840
  86.5 2.2 %row_update.1 = (f32[400,256]{1,0:T(8,128)}, f32[1,256]{1,0:T(1,128)}, f32[5,400]{1,0:T(8,128)}, f32[1,5]{1,0:T(1,128)}) custom-call(f32[400,256]{1,0:T(8,128)} %bitcast.9, f32[1,256]{1,0:T(1,128)} %bitcast.10, f32[5,400]{1,0:T(8,128)} %rel.1, f32[1,5]{1,0:T(1,128)} %bitcast.11, f32[400,256]{1,0:T(8,128)} %get-tuple-element.10.ent_grad, ...), custom_call_target="tpu_custom_call" | custom-call | tf_op jit(solution)/shard_map/row_update/pallas_call | solution.py:856
